TPU v7x, 128 devices: a whole 4x4x4 slice. The times are simulated.
128 devices in a mesh: row: 8 (over y, core), col: 16 (over z, x).
Axes of the slice: x: 4, y: 4, z: 4, core: 2. Of those that a mesh axis runs over, the one named last changes fastest.
Arguments:
- block_x: float32 [64, 98304], P(None, ('row', 'col')), may hold values from -6 to 6
- block_p: float32 [64, 98304], P(None, ('row', 'col')), may hold values from -6 to 6
- tile_rows: int32 [8, 16, 576], P('row', 'col'), may hold values from 0 to 95, as said below
- tile_cols: int32 [8, 16, 576], P('row', 'col'), may hold values from 0 to 47, as said below
- tile_count: int32 [8, 16], P('row', 'col'), may hold values from 1 to 576, as said below
- tile_vals: bfloat16 [8, 16, 576, 128, 128], P('row', 'col'), may hold values from -0.125 to 0.125
Outputs:
- residual: float32 [64, 98304], P(None, ('row', 'col'))
- image_r: float32 [64, 98304], P(None, ('row', 'col'))
- gram_a: float32 [192, 192], replicated
- gram_b: float32 [192, 192], replicated
Inputs may be any that keep to these rules, and one draw needn't show every extreme that they name: `tile_rows`: within one grid cell the live slots name distinct tiles, all with i <= j; slots at and beyond the cell's count are ignored. `tile_cols`: paired with tile_rows slot by slot. `tile_count`: some grid cell is full in every draw.
All inputs are finite; a program needn't handle non-finite values.
Results may differ from a plain program's by a relative error of at most 0.0035.
Values may be sent and summed in bfloat16 or wider, within the bound.
A program may use at most 128 MiB of HBM per device.

v0:
```python
import math

import jax
import jax.numpy as jnp
from jax import lax
from jax.sharding import PartitionSpec as P


def apply_graph(vectors, tile_rows, tile_cols, live_count, tile_vals):
    vec_width = vectors.shape[0]
    tile_size = tile_vals.shape[-1]
    row_range = lax.all_gather(vectors, "col", axis=1, tiled=True)
    col_group = lax.all_gather(vectors, "row", axis=1, tiled=True)
    row_blocks = row_range.reshape(vec_width, -1, tile_size)
    col_blocks = col_group.reshape(vec_width, -1, tile_size)
    group_size = math.gcd(tile_vals.shape[0], 64)
    offsets = jnp.arange(group_size, dtype=jnp.int32)
    turn_count = (live_count + group_size - 1) // group_size

    def slot_group(turn_index):
        first_slot = turn_index * group_size
        row_index = lax.dynamic_slice_in_dim(tile_rows, first_slot, group_size)
        col_index = lax.dynamic_slice_in_dim(tile_cols, first_slot, group_size)
        values = lax.dynamic_slice_in_dim(tile_vals, first_slot, group_size, 0)
        live_slots = first_slot + offsets < live_count
        return (row_index, col_index, values, live_slots)

    def turn(turn_index, totals):
        row_totals, col_totals = totals
        row_index, col_index, values, live_slots = slot_group(turn_index)
        values = jnp.where(live_slots[:, None, None], values, jnp.zeros_like(values))
        col_inputs = jnp.take(col_blocks, col_index, axis=1)
        row_inputs = jnp.take(row_blocks, row_index, axis=1)
        forward = jnp.einsum("wgb,gab->wga", col_inputs, values, preferred_element_type=jnp.float32)
        backward = jnp.einsum(
            "wga,gab->wgb", row_inputs, values, preferred_element_type=jnp.float32
        )
        return (row_totals.at[:, row_index].add(forward), col_totals.at[:, col_index].add(backward))

    start_rows = jnp.zeros(row_blocks.shape, jnp.float32)
    start_cols = jnp.zeros(col_blocks.shape, jnp.float32)
    row_totals, col_totals = lax.fori_loop(0, turn_count, turn, (start_rows, start_cols))
    own_rows = lax.psum_scatter(
        row_totals.reshape(vec_width, -1), "col", scatter_dimension=1, tiled=True
    )
    own_cols = lax.psum_scatter(
        col_totals.reshape(vec_width, -1), "row", scatter_dimension=1, tiled=True
    )
    return own_rows + own_cols


def per_device(block_x, block_p, tile_rows, tile_cols, tile_count, tile_vals):
    highest = lax.Precision.HIGHEST
    width_k = block_x.shape[0]
    node_count = block_x.shape[1] * lax.axis_size("row") * lax.axis_size("col")
    slot_rows = tile_rows[0, 0]
    slot_cols = tile_cols[0, 0]
    live_count = tile_count[0, 0]
    slot_vals = tile_vals[0, 0]

    def product(left, right):
        return (
            jnp.dot(left, right.T, precision=highest, preferred_element_type=jnp.float32)
            / node_count
        )

    gram_x = lax.psum(product(block_x, block_x), ("row", "col"))
    cholesky_factor = jnp.linalg.cholesky(gram_x)
    orthonormal = lax.linalg.triangular_solve(cholesky_factor, block_x, left_side=True, lower=True)
    ortho_low = orthonormal.astype(jnp.bfloat16)
    dir_low = block_p.astype(jnp.bfloat16)
    both_images = apply_graph(
        jnp.concatenate([ortho_low, dir_low], axis=0), slot_rows, slot_cols, live_count, slot_vals
    )
    image_x = both_images[:width_k]
    image_p = both_images[width_k:]
    rayleigh = lax.psum(product(orthonormal, image_x), ("row", "col"))
    residual = image_x - jnp.dot(
        rayleigh.T, orthonormal, precision=highest, preferred_element_type=jnp.float32
    )
    residual_low = residual.astype(jnp.bfloat16)
    image_r = apply_graph(residual_low, slot_rows, slot_cols, live_count, slot_vals)
    basis = jnp.concatenate([orthonormal, residual, block_p], axis=0)
    images = jnp.concatenate([image_x, image_r, image_p], axis=0)
    gram_a, gram_b = lax.psum((product(basis, images), product(basis, basis)), ("row", "col"))
    return (residual, image_r, gram_a, gram_b)


def solution(mesh):
    in_specs = (
        P(None, ("row", "col")),
        P(None, ("row", "col")),
        P("row", "col", None),
        P("row", "col", None),
        P("row", "col"),
        P("row", "col", None, None, None),
    )
    out_specs = (P(None, ("row", "col")), P(None, ("row", "col")), P(), P())
    return jax.shard_map(
        per_device, mesh=mesh, in_specs=in_specs, out_specs=out_specs, check_vma=False
    )
```

profile of v0, /device:TPU:1, one launch (start us, length us, event | category | flops | bytes accessed | tf_op | source)
XLA Modules:
  0.0 1301.9 jit_solution(9293041823528149920)
XLA Ops:
  8.4 68.9 %psum.28 = f32[64,64]{0,1:T(8,128)S(1)} all-reduce(f32[64,64]{0,1:T(8,128)S(1)} %convolution_multiply_fusion.3), channel_id=1, replica_groups=mesh['row'=8,'col'=16] {'row','col'}, use_global_device_ids=true, to_apply=%region_0.0 | all-reduce | flops 4096 | bytes 32768 | tf_op jit(solution)/shard_map/psum | solution.py:67
  93.1 19.8 %all-gather.4.cloned.1.call-done = bf16[128,6144]{1,0:T(8,128)(2,1)} async-done(((bf16[128,768]{1,0:T(8,128)(2,1)}), bf16[128,6144]{1,0:T(8,128)(2,1)}) %all-gather.4.cloned.1.call-update) | async-done | bytes 1572880 | tf_op jit(solution)/shard_map/all_gather | solution.py:13
  115.9 47.5 %all-gather.6.cloned.1.call-done = bf16[128,12288]{1,0:T(8,128)(2,1)} async-done(((bf16[128,768]{1,0:T(8,128)(2,1)}), bf16[128,12288]{1,0:T(8,128)(2,1)}) %all-gather.6.cloned.1.call-update) | async-done | bytes 3145744 | tf_op jit(solution)/shard_map/all_gather | solution.py:12
  171.6 290.5 %while.26 = (s32[]{:T(128)}, f32[128,96,128]{2,0,1:T(8,128)}, f32[128,48,128]{2,0,1:T(8,128)S(1)}, s32[]{:T(128)}, s32[576]{0:T(1024)S(1)}, /*index=5*/s32[]{:T(...) while((s32[]{:T(128)}, f32[128,96,128]{2,0,1:T(8,128)}, ...), condition=%wide.region_6.7_spmd.clone, body=%wide.region_3.6_spmd.clone.sunk | while | flops 543165312 | bytes 50343056 | solution.py:42
  181.7 13.6 %scatter_fusion = f32[128,96,128]{2,0,1:T(8,128)} fusion(f32[128,96,128]{2,0,1:T(8,128)} %get-tuple-element.407, s32[64]{0:T(128)S(1)} %get-tuple-element.374, f32[64,128,128]{2,1,0:T(8,128)} %fusion.80), kind=kCustom, calls=%fused_computation.4.clone.clone.1 | custom fusion | flops 1048576 | bytes 12583168 | tf_op jit(solution)/shard_map/while/body/scatter-add | solution.py:38
  223.2 13.5 %scatter_fusion = f32[128,96,128]{2,0,1:T(8,128)} fusion(f32[128,96,128]{2,0,1:T(8,128)} %get-tuple-element.407, s32[64]{0:T(128)S(1)} %get-tuple-element.374, f32[64,128,128]{2,1,0:T(8,128)} %fusion.80), kind=kCustom, calls=%fused_computation.4.clone.clone.1 | custom fusion | flops 1048576 | bytes 12583168 | tf_op jit(solution)/shard_map/while/body/scatter-add | solution.py:38
  264.6 13.7 %scatter_fusion = f32[128,96,128]{2,0,1:T(8,128)} fusion(f32[128,96,128]{2,0,1:T(8,128)} %get-tuple-element.407, s32[64]{0:T(128)S(1)} %get-tuple-element.374, f32[64,128,128]{2,1,0:T(8,128)} %fusion.80), kind=kCustom, calls=%fused_computation.4.clone.clone.1 | custom fusion | flops 1048576 | bytes 12583168 | tf_op jit(solution)/shard_map/while/body/scatter-add | solution.py:38
  306.2 13.6 %scatter_fusion = f32[128,96,128]{2,0,1:T(8,128)} fusion(f32[128,96,128]{2,0,1:T(8,128)} %get-tuple-element.407, s32[64]{0:T(128)S(1)} %get-tuple-element.374, f32[64,128,128]{2,1,0:T(8,128)} %fusion.80), kind=kCustom, calls=%fused_computation.4.clone.clone.1 | custom fusion | flops 1048576 | bytes 12583168 | tf_op jit(solution)/shard_map/while/body/scatter-add | solution.py:38
  347.7 13.6 %scatter_fusion = f32[128,96,128]{2,0,1:T(8,128)} fusion(f32[128,96,128]{2,0,1:T(8,128)} %get-tuple-element.407, s32[64]{0:T(128)S(1)} %get-tuple-element.374, f32[64,128,128]{2,1,0:T(8,128)} %fusion.80), kind=kCustom, calls=%fused_computation.4.clone.clone.1 | custom fusion | flops 1048576 | bytes 12583168 | tf_op jit(solution)/shard_map/while/body/scatter-add | solution.py:38
  389.2 13.6 %scatter_fusion = f32[128,96,128]{2,0,1:T(8,128)} fusion(f32[128,96,128]{2,0,1:T(8,128)} %get-tuple-element.407, s32[64]{0:T(128)S(1)} %get-tuple-element.374, f32[64,128,128]{2,1,0:T(8,128)} %fusion.80), kind=kCustom, calls=%fused_computation.4.clone.clone.1 | custom fusion | flops 1048576 | bytes 12583168 | tf_op jit(solution)/shard_map/while/body/scatter-add | solution.py:38
  430.7 13.6 %scatter_fusion = f32[128,96,128]{2,0,1:T(8,128)} fusion(f32[128,96,128]{2,0,1:T(8,128)} %get-tuple-element.407, s32[64]{0:T(128)S(1)} %get-tuple-element.374, f32[64,128,128]{2,1,0:T(8,128)} %fusion.80), kind=kCustom, calls=%fused_computation.4.clone.clone.1 | custom fusion | flops 1048576 | bytes 12583168 | tf_op jit(solution)/shard_map/while/body/scatter-add | solution.py:38
  470.3 106.5 %reduce-scatter.7.cloned.1.call-done = f32[128,768]{1,0:T(8,128)} async-done(((f32[128,6144]{1,0:T(8,128)}), f32[128,768]{1,0:T(8,128)}) %reduce-scatter.7.cloned.1.call-update) | async-done | bytes 393232 | tf_op jit(solution)/shard_map/reduce_scatter | solution.py:46
  576.8 85.4 %reduce-scatter.5.cloned.1.call-done = f32[128,768]{1,0:T(8,128)} async-done(((f32[128,12288]{1,0:T(8,128)}), f32[128,768]{1,0:T(8,128)}) %reduce-scatter.5.cloned.1.call-update) | async-done | bytes 393232 | tf_op jit(solution)/shard_map/reduce_scatter | solution.py:43
  663.7 65.7 %psum.29 = f32[64,64]{0,1:T(8,128)S(1)} all-reduce(f32[64,64]{0,1:T(8,128)S(1)} %convolution_multiply_fusion.2), channel_id=1, replica_groups=mesh['row'=8,'col'=16] {'row','col'}, use_global_device_ids=true, to_apply=%region_9.10 | all-reduce | flops 4096 | bytes 32768 | tf_op jit(solution)/shard_map/psum | solution.py:77
  730.5 14.3 %all_gather.14 = bf16[64,6144]{1,0:T(8,128)(2,1)S(1)} all-gather(bf16[64,768]{1,0:T(8,128)(2,1)} %get-tuple-element.250), channel_id=1, replica_groups=mesh['row'=8,'col'=16] {'row'}, dimensions={1}, use_global_device_ids=true | all-gather | bytes 884736 | tf_op jit(solution)/shard_map/all_gather | solution.py:13
  745.9 24.0 %all-gather.8.cloned.1.call-done = bf16[64,12288]{1,0:T(8,128)(2,1)} async-done(((bf16[64,768]{1,0:T(8,128)(2,1)}), bf16[64,12288]{1,0:T(8,128)(2,1)}) %all-gather.8.cloned.1.call-update) | async-done | bytes 1572880 | tf_op jit(solution)/shard_map/all_gather | solution.py:12
  776.3 198.6 %while.27 = (s32[]{:T(128)}, f32[64,96,128]{2,0,1:T(8,128)}, f32[64,48,128]{2,0,1:T(8,128)}, s32[]{:T(128)}, s32[576]{0:T(1024)S(1)}, /*index=5*/s32[]{:T(128)},...) while((s32[]{:T(128)}, f32[64,96,128]{2,0,1:T(8,128)}, ...), condition=%wide.region_13.14_spmd.clone, body=%wide.region_10.13_spmd.clone.sunk | while | flops 272632704 | bytes 27274384 | solution.py:42
  782.1 9.0 scatter_fusion.2
  795.7 9.0 scatter_fusion.3
  824.0 9.0 scatter_fusion.3
  838.8 9.0 scatter_fusion.2
  852.3 9.0 scatter_fusion.3
  880.7 9.0 scatter_fusion.3
  895.5 9.0 scatter_fusion.2
  909.0 9.0 scatter_fusion.3
  923.9 9.0 scatter_fusion.2
  937.4 9.1 scatter_fusion.3
  952.4 9.0 scatter_fusion.2
  965.9 9.0 scatter_fusion.3
  982.1 79.9 %reduce-scatter.11.cloned.1.call-done = f32[64,768]{1,0:T(8,128)} async-done(((f32[64,6144]{1,0:T(8,128)}), f32[64,768]{1,0:T(8,128)}) %reduce-scatter.11.cloned.1.call-update) | async-done | bytes 196624 | tf_op jit(solution)/shard_map/reduce_scatter | solution.py:46
  1062.0 79.3 %reduce-scatter.9.cloned.1.call-done = f32[64,768]{1,0:T(8,128)} async-done(((f32[64,12288]{1,0:T(8,128)}), f32[64,768]{1,0:T(8,128)}) %reduce-scatter.9.cloned.1.call-update) | async-done | bytes 196624 | tf_op jit(solution)/shard_map/reduce_scatter | solution.py:43
  1143.7 148.1 %all-reduce.3.cloned.1.call-done = (f32[192,192]{1,0:T(8,128)}, f32[192,192]{1,0:T(8,128)}) async-done(((f32[192,192]{1,0:T(8,128)}, f32[192,192]{1,0:T(8,128)}), (f32[192,192]{1,0:T(8,128)}, f32[192,192]{1,0:T(8,128)})) %all-reduce.3.cloned.1.call-update) | async-done | bytes 294928 | tf_op jit(solution)/shard_map/psum | solution.py:85
  (191 shorter events, 343.5 us)
Async XLA Ops:
  7.2 0.9 copy-start
  7.2 85.8 %copy-start.8 = (s32[1,1,576]{2,1,0:T(1,128)S(1)}, s32[1,1,576]{2,1,0:T(1,128)}, u32[]{:S(2)}) copy-start(s32[1,1,576]{2,1,0:T(1,128)} %param.12) | copy-start | bytes 6916
  7.2 85.8 %copy-start.9 = (s32[1,1,576]{2,1,0:T(1,128)S(1)}, s32[1,1,576]{2,1,0:T(1,128)}, u32[]{:S(2)}) copy-start(s32[1,1,576]{2,1,0:T(1,128)} %param.13) | copy-start | bytes 6916
  7.2 105.7 %all-gather.4.cloned.1.call-start = ((), (), s32[]{:S(2)}) async-start(), calls=%async_computation.4 | async-start | bytes 1769472 | tf_op jit(solution)/shard_map/all_gather | solution.py:13
  91.5 71.8 %all-gather.6.cloned.1.call-start = ((), (), s32[]{:S(2)}) async-start(), calls=%async_computation.5 | async-start | bytes 3342336 | tf_op jit(solution)/shard_map/all_gather | solution.py:12
  92.3 484.5 %reduce-scatter.7.cloned.1.call-start = ((), (), s32[]{:S(2)}) async-start(), calls=%async_computation.7 | async-start | bytes 3538944 | tf_op jit(solution)/shard_map/reduce_scatter | solution.py:46
  464.1 198.2 %reduce-scatter.5.cloned.1.call-start = ((), (), s32[]{:S(2)}) async-start(), calls=%async_computation.6 | async-start | bytes 6684672 | tf_op jit(solution)/shard_map/reduce_scatter | solution.py:43
  470.2 299.7 %all-gather.8.cloned.1.call-start = ((), (), s32[]{:S(2)}) async-start(), calls=%async_computation.8 | async-start | bytes 1671168 | tf_op jit(solution)/shard_map/all_gather | solution.py:12
  663.4 109.5 %copy-start.3 = (f32[128,768]{1,0:T(8,128)}, f32[128,768]{1,0:T(8,128)S(1)}, u32[]{:S(2)}) copy-start(f32[128,768]{1,0:T(8,128)S(1)} %add.116) | copy-start | bytes 1179652
  730.4 331.5 %reduce-scatter.11.cloned.1.call-start = ((), (), s32[]{:S(2)}) async-start(), calls=%async_computation.10 | async-start | bytes 1769472 | tf_op jit(solution)/shard_map/reduce_scatter | solution.py:46
  974.9 2.9 copy-start.2
  977.7 163.6 %reduce-scatter.9.cloned.1.call-start = ((), (), s32[]{:S(2)}) async-start(), calls=%async_computation.9 | async-start | bytes 3342336 | tf_op jit(solution)/shard_map/reduce_scatter | solution.py:43
  979.7 0.9 copy-start.5
  979.7 1.0 copy-start.6
  979.7 2.4 copy-start.4
  979.7 312.2 %all-reduce.3.cloned.1.call-start = ((), (), s32[]{:S(2)}) async-start(), calls=%async_computation.11 | async-start | bytes 786432 | tf_op jit(solution)/shard_map/psum | solution.py:85
  980.7 314.4 %copy-start.1 = (f32[64,768]{1,0:T(8,128)S(1)}, f32[64,768]{1,0:T(8,128)}, u32[]{:S(2)}) copy-start(f32[64,768]{1,0:T(8,128)} %param.10) | copy-start | bytes 589828
  1142.4 152.7 %copy-start.7 = (f32[64,768]{1,0:T(8,128)}, f32[64,768]{1,0:T(8,128)S(1)}, u32[]{:S(2)}) copy-start(f32[64,768]{1,0:T(8,128)S(1)} %add.117) | copy-start | bytes 589828
Sparse Core Ops, SparseCore 0:
  91.7 21.1 all-gather.3
  115.6 47.6 all-gather.5
  464.2 112.5 reduce-scatter.6
  580.1 82.1 reduce-scatter.4
  730.6 39.2 all-gather.7
  977.9 84.0 reduce-scatter.10
  1065.3 75.9 reduce-scatter.8
  1146.7 145.1 all-reduce.2
where the time goes:
time: 1310 us; the launch traced here: 1300 us
  waiting for transfers between devices  591 us (45%)
  other arithmetic  309 us (24%)
  blocking collectives  149 us (11%)
  local copies, waits for them, and re-layouts  118 us (9%)
  matrix products  118 us (9%)
  between operations  15 us (1%)
    reduce_scatter x2, waiting for transfers between devices, apply_graph(): lax.psum_scatter(col_totals.reshape(vec_width, -1), 'row', scatter_dimens...  186 us
    reduce_scatter x2, waiting for transfers between devices, apply_graph(): lax.psum_scatter(row_totals.reshape(vec_width, -1), 'col', scatter_dimens...  165 us
    scatter-add x14, other arithmetic, turn(): row_totals.at[:, row_index].add(forward)  158 us
    psum x1, waiting for transfers between devices, per_device(): lax.psum((product(basis, images), product(basis, basis)), ('row', 'col'))  148 us
    scatter-add x14, other arithmetic, turn(): col_totals.at[:, col_index].add(backward)  125 us
    all_gather x2, waiting for transfers between devices, apply_graph(): row_range = lax.all_gather(vectors, 'col', axis=1, tiled=True)  71.4 us
    psum x1, blocking collectives, per_device(): gram_x = lax.psum(product(block_x, block_x), ('row', 'col'))  68.9 us
    psum x1, blocking collectives, per_device(): rayleigh = lax.psum(product(orthonormal, image_x), ('row', 'col'))  65.7 us
  transfers between devices with their start and end apart: 8, of which 8 were waited for; matrix products, arithmetic and copies ran while one was open for 1% of the time, Pallas kernels for 0%

commit v1 on v0

v1 whole, which is shorter than its diff:
```python
import functools

import jax
import jax.numpy as jnp
from jax import lax
from jax.experimental import pallas as pl
from jax.experimental.pallas import tpu as pltpu
from jax.sharding import PartitionSpec as P

F32 = jnp.float32
BF16 = jnp.bfloat16
TILE = 128
HIGHEST = lax.Precision.HIGHEST
MESH = pl.DeviceIdType.MESH
VMEM_LIMIT = 56 * 2**20
GROUP = 48
UNROLL = 16
X_WIRE = F32
R_WIRE = BF16


def dot_nt(left, right):
    return lax.dot_general(
        left, right, (((1,), (1,)), ((), ())), precision=HIGHEST, preferred_element_type=F32
    )


def dot_tn(left, right):
    return lax.dot_general(
        left, right, (((0,), (0,)), ((), ())), precision=HIGHEST, preferred_element_type=F32
    )


def dot_nn(left, right):
    return lax.dot_general(
        left, right, (((1,), (0,)), ((), ())), precision=HIGHEST, preferred_element_type=F32
    )


class Line:
    def __init__(self, name, size):
        self.name, self.size = name, size
        self.me = lax.axis_index(name)

    def ahead(self, k):
        return lax.rem(self.me + k, self.size)

    def behind(self, k):
        return lax.rem(self.me + self.size - k, self.size)

    def greet(self, barrier):
        for k in range(1, self.size):
            pl.semaphore_signal(
                barrier, inc=1, device_id={self.name: self.ahead(k)}, device_id_type=MESH
            )

    def copies(self, source, target, send_sem, recv_sem):
        return [
            pltpu.make_async_remote_copy(
                src_ref=source(self.ahead(k)),
                dst_ref=target(self.me),
                send_sem=send_sem.at[k],
                recv_sem=recv_sem.at[k],
                device_id={self.name: self.ahead(k)},
                device_id_type=MESH,
            )
            for k in range(1, self.size)
        ]

    def arrivals(self, source, target, send_sem, recv_sem):
        return [
            pltpu.make_async_remote_copy(
                src_ref=source(self.ahead(k)),
                dst_ref=target(self.behind(k)),
                send_sem=send_sem.at[k],
                recv_sem=recv_sem.at[k],
                device_id={self.name: self.ahead(k)},
                device_id_type=MESH,
            )
            for k in range(1, self.size)
        ]


class Exchange:
    def __init__(self, line, source, target, sems):
        self.sent = line.copies(source, target, sems.at[0], sems.at[1])
        self.come = line.arrivals(source, target, sems.at[0], sems.at[1])

    def start(self):
        for c in self.sent:
            c.start()
        return self

    def wait_recv(self):
        for c in self.come:
            c.wait_recv()
        return self

    def wait_send(self):
        for c in self.sent:
            c.wait_send()
        return self


def enter(rows, cols):
    barrier = pltpu.get_barrier_semaphore()
    rows.greet(barrier)
    cols.greet(barrier)
    pl.semaphore_wait(barrier, rows.size + cols.size - 2)


def sum_slots(ref, count):
    total = ref[0]
    for j in range(1, count):
        total = total + ref[j]
    return total


def all_reduce(rows, cols, part, first, second, row_sems, col_sems):
    first[rows.me] = part
    one = Exchange(rows, lambda p: first.at[rows.me], lambda s: first.at[s], row_sems)
    one.start().wait_recv()
    second[cols.me] = sum_slots(first, rows.size)
    two = Exchange(cols, lambda p: second.at[cols.me], lambda s: second.at[s], col_sems)
    two.start().wait_recv()
    total = sum_slots(second, cols.size)
    one.wait_send()
    two.wait_send()
    return total


def factor(gram):
    k_width = gram.shape[0]
    row_id = lax.broadcasted_iota(jnp.int32, (k_width, k_width), 0)
    col_id = lax.broadcasted_iota(jnp.int32, (k_width, k_width), 1)
    eye = jnp.where(row_id == col_id, 1.0, 0.0).astype(F32)
    work = jnp.concatenate([gram, eye], axis=1)
    down = lax.broadcasted_iota(jnp.int32, (k_width, 2 * k_width), 0)
    pivots = []
    for k in range(k_width):
        pivot_row = work[k : k + 1, :]
        pivot = work[k : k + 1, k : k + 1]
        pivots.append(pivot)
        if k + 1 < k_width:
            ratio = work[:, k : k + 1] / pivot
            work = work - jnp.where(down > k, ratio * pivot_row, 0.0)
    scale = lax.rsqrt(jnp.concatenate(pivots, axis=0))
    return work[:, k_width:] * scale


def first_kernel(
    n_row, n_col, node_count, x_ref, p_ref, ortho_ref, vrow_ref, vcol_ref,
    low, first, second, ar_row, ar_col, p_row, p_col, x_row, x_col, own,
):
    rows, cols = Line("row", n_row), Line("col", n_col)
    k_width, mine = x_ref.shape
    blocks = mine // TILE
    enter(rows, cols)

    for b in range(blocks):
        low[b, k_width:, :] = p_ref[:, b * TILE : (b + 1) * TILE].astype(BF16)

    gram = dot_nt(x_ref[...], x_ref[...]) / node_count
    zero = jnp.zeros((k_width, TILE - k_width), F32)
    part = jnp.concatenate([gram, zero], axis=1)

    x_half, p_half = pl.ds(0, k_width), pl.ds(k_width, k_width)

    def gather(line, out, half, sems):
        return Exchange(
            line, lambda p: low.at[:, half, :], lambda s: out.at[s, :, half, :], sems
        )

    p_moves = [gather(cols, vrow_ref, p_half, p_col), gather(rows, vcol_ref, p_half, p_row)]
    x_moves = [gather(cols, vrow_ref, x_half, x_col), gather(rows, vcol_ref, x_half, x_row)]
    for m in p_moves:
        m.start()
    gram = all_reduce(rows, cols, part, first, second, ar_row, ar_col)[:, :k_width]
    ortho = dot_nn(factor(gram), x_ref[...])
    ortho_ref[...] = ortho
    for b in range(blocks):
        low[b, :k_width, :] = ortho[:, b * TILE : (b + 1) * TILE].astype(BF16)
    for m in x_moves:
        m.start()
    here = [
        pltpu.make_async_copy(low, vrow_ref.at[cols.me], own.at[0]),
        pltpu.make_async_copy(low, vcol_ref.at[rows.me], own.at[1]),
    ]
    for c in here:
        c.start()
    for m in p_moves + x_moves:
        m.wait_recv()
    for m in p_moves + x_moves:
        m.wait_send()
    for c in here:
        c.wait()


def apply_kernel(
    splits, rows_ref, cols_ref, count_ref, vrow_ref, vcol_ref, tile_ref, *rest
):
    outs, (row_acc, col_acc) = rest[:-2], rest[-2:]
    row_blocks, col_blocks = vrow_ref.shape[0], vcol_ref.shape[0]
    step = pl.program_id(0)

    @pl.when(step == 0)
    def _():
        row_acc[...] = jnp.zeros_like(row_acc)
        col_acc[...] = jnp.zeros_like(col_acc)

    count = count_ref[0]
    base = step * GROUP
    todo = jnp.clip(count - base, 0, GROUP)

    def body(turn, carry):
        for u in range(UNROLL):
            slot = turn * UNROLL + u
            live = base + slot < count
            a = rows_ref[base + slot]
            b = cols_ref[base + slot]
            tile = tile_ref[slot]
            forward = lax.dot_general(
                vcol_ref[b], tile, (((1,), (1,)), ((), ())), preferred_element_type=F32
            )
            row_acc[jnp.where(live, a, row_blocks)] += forward
            backward = lax.dot_general(
                vrow_ref[a], tile, (((1,), (0,)), ((), ())), preferred_element_type=F32
            )
            col_acc[jnp.where(live, b, col_blocks)] += backward
        return carry

    lax.fori_loop(0, (todo + UNROLL - 1) // UNROLL, body, 0)

    @pl.when(step == pl.num_programs(0) - 1)
    def _():
        at = 0
        for i, width in enumerate(splits):
            for out, acc, n in ((outs[2 * i], row_acc, row_blocks), (outs[2 * i + 1], col_acc, col_blocks)):
                out[...] = acc[:n, at : at + width, :].astype(out.dtype)
            at += width


def apply_graph(tile_rows, tile_cols, count, vrow, vcol, tile_vals, splits):
    width = vrow.shape[1]
    slots = tile_vals.shape[0]
    n_r, n_c = vrow.shape[0], vcol.shape[0]
    whole = lambda n, w: pl.BlockSpec((n, w, TILE), lambda g, *_: (0, 0, 0))
    out_shape, out_specs = [], []
    for w, wire in splits:
        for n in (n_r, n_c):
            out_shape.append(jax.ShapeDtypeStruct((n, w, TILE), wire))
            out_specs.append(whole(n, w))
    flops = 4 * slots * width * TILE * TILE
    return pl.pallas_call(
        functools.partial(apply_kernel, [w for w, _ in splits]),
        grid_spec=pltpu.PrefetchScalarGridSpec(
            num_scalar_prefetch=3,
            grid=(slots // GROUP,),
            in_specs=[
                whole(n_r, width),
                whole(n_c, width),
                pl.BlockSpec((GROUP, TILE, TILE), lambda g, *_: (g, 0, 0)),
            ],
            out_specs=out_specs,
            scratch_shapes=[
                pltpu.VMEM((n_r + 1, width, TILE), F32),
                pltpu.VMEM((n_c + 1, width, TILE), F32),
            ],
        ),
        out_shape=out_shape,
        compiler_params=pltpu.CompilerParams(vmem_limit_bytes=VMEM_LIMIT),
        cost_estimate=pl.CostEstimate(
            flops=flops, bytes_accessed=2 * slots * TILE * TILE, transcendentals=0
        ),
    )(tile_rows, tile_cols, count, vrow, vcol, tile_vals)


class Scatter:
    def __init__(self, rows, cols, by_row, by_col, row_in, col_in, sems, own):
        row_sems, col_sems = sems
        blocks = row_in.shape[1]
        self.row_in, self.col_in = row_in, col_in
        self.n_col, self.n_row = cols.size, rows.size
        part = lambda ref: lambda p: ref.at[pl.ds(p * blocks, blocks)]
        self.moves = [
            Exchange(cols, part(by_row), lambda s: row_in.at[s], col_sems),
            Exchange(rows, part(by_col), lambda s: col_in.at[s], row_sems),
        ]
        self.here = [
            pltpu.make_async_copy(part(by_row)(cols.me), row_in.at[cols.me], own.at[0]),
            pltpu.make_async_copy(part(by_col)(rows.me), col_in.at[rows.me], own.at[1]),
        ]

    def start(self):
        for m in self.moves + self.here:
            m.start()

    def finish(self, image_ref):
        for m in self.moves:
            m.wait_recv()
        for c in self.here:
            c.wait()
        for b in range(self.row_in.shape[1]):
            total = self.row_in[0, b].astype(F32)
            for j in range(1, self.n_col):
                total = total + self.row_in[j, b].astype(F32)
            for j in range(self.n_row):
                total = total + self.col_in[j, b].astype(F32)
            image_ref[:, b * TILE : (b + 1) * TILE] = total

    def wait_send(self):
        for m in self.moves:
            m.wait_send()


def middle_kernel(
    n_row, n_col, node_count, ortho_ref, xr_ref, xc_ref, pr_ref, pc_ref,
    residual_ref, image_x_ref, image_p_ref, vrow_ref, vcol_ref,
    xr_in, xc_in, pr_in, pc_in, low, first, second,
    x_row, x_col, p_row, p_col, ar_row, ar_col, g_row, g_col, own,
):
    rows, cols = Line("row", n_row), Line("col", n_col)
    k_width, mine = ortho_ref.shape
    blocks = mine // TILE
    enter(rows, cols)
    x_sum = Scatter(rows, cols, xr_ref, xc_ref, xr_in, xc_in, (x_row, x_col), own.at[0])
    p_sum = Scatter(rows, cols, pr_ref, pc_ref, pr_in, pc_in, (p_row, p_col), own.at[1])
    x_sum.start()
    x_sum.finish(image_x_ref)
    ortho = ortho_ref[...]
    part = dot_nt(ortho, image_x_ref[...]) / node_count
    zero = jnp.zeros((k_width, TILE - k_width), F32)
    part = jnp.concatenate([part, zero], axis=1)
    rayleigh = all_reduce(rows, cols, part, first, second, ar_row, ar_col)[:, :k_width]
    residual = image_x_ref[...] - dot_tn(rayleigh, ortho)
    residual_ref[...] = residual
    for b in range(blocks):
        low[b] = residual[:, b * TILE : (b + 1) * TILE].astype(BF16)
    gathers = [
        Exchange(cols, lambda p: low, lambda s: vrow_ref.at[s], g_col),
        Exchange(rows, lambda p: low, lambda s: vcol_ref.at[s], g_row),
    ]
    here = [
        pltpu.make_async_copy(low, vrow_ref.at[cols.me], own.at[2, 0]),
        pltpu.make_async_copy(low, vcol_ref.at[rows.me], own.at[2, 1]),
    ]
    for c in gathers + here:
        c.start()
    p_sum.start()
    for c in gathers:
        c.wait_recv()
    p_sum.finish(image_p_ref)
    for c in here:
        c.wait()
    for c in gathers + [x_sum, p_sum]:
        c.wait_send()


def last_kernel(
    n_row, n_col, node_count, ortho_ref, residual_ref, p_ref, image_x_ref, image_p_ref,
    rr_ref, rc_ref, image_r_ref, gram_a_ref, gram_b_ref,
    rr_in, rc_in, whole, done, first, second, r_row, r_col, s_row, s_col, g_row, own,
):
    rows, cols = Line("row", n_row), Line("col", n_col)
    k_width = ortho_ref.shape[0]
    full = 3 * k_width
    share = full // n_row
    enter(rows, cols)
    r_sum = Scatter(rows, cols, rr_ref, rc_ref, rr_in, rc_in, (r_row, r_col), own)
    r_sum.start()
    basis = jnp.concatenate([ortho_ref[...], residual_ref[...], p_ref[...]], axis=0)
    whole[:, full:] = dot_nt(basis, basis) / node_count
    r_sum.finish(image_r_ref)
    images = jnp.concatenate([image_x_ref[...], image_r_ref[...], image_p_ref[...]], axis=0)
    whole[:, :full] = dot_nt(basis, images) / node_count

    def mine(p):
        return pl.ds(pl.multiple_of(p * share, 8), share)

    first[rows.me] = whole[mine(rows.me), :]
    one = Exchange(rows, lambda p: whole.at[mine(p)], lambda s: first.at[s], s_row)
    one.start().wait_recv()
    second[cols.me] = sum_slots(first, n_row)
    two = Exchange(cols, lambda p: second.at[cols.me], lambda s: second.at[s], s_col)
    two.start().wait_recv()
    one.wait_send()
    done[mine(rows.me), :] = sum_slots(second, n_col)
    three = Exchange(
        rows, lambda p: done.at[mine(rows.me)], lambda s: done.at[mine(s)], g_row
    )
    three.start().wait_recv()
    gram_a_ref[...] = done[:, :full]
    gram_b_ref[...] = done[:, full:]
    two.wait_send()
    three.wait_send()
    r_sum.wait_send()


def per_device(block_x, block_p, tile_rows, tile_cols, tile_count, tile_vals):
    n_row, n_col = lax.axis_size("row"), lax.axis_size("col")
    k_width, mine = block_x.shape
    node_count = mine * n_row * n_col
    blocks = mine // TILE
    slots = tile_vals.shape[2]
    slot_rows = tile_rows.reshape(slots)
    slot_cols = tile_cols.reshape(slots)
    count = tile_count.reshape(1)
    vals = tile_vals.reshape(slots, TILE, TILE)
    vmem = pl.BlockSpec(memory_space=pltpu.VMEM)
    anywhere = pl.BlockSpec(memory_space=pl.ANY)
    row_sems = pltpu.SemaphoreType.DMA((2, n_row))
    col_sems = pltpu.SemaphoreType.DMA((2, n_col))
    shape = jax.ShapeDtypeStruct
    params = lambda i: pltpu.CompilerParams(
        collective_id=i, has_side_effects=True, vmem_limit_bytes=VMEM_LIMIT
    )
    local = shape((k_width, mine), F32)

    ortho, vrow, vcol = pl.pallas_call(
        functools.partial(first_kernel, n_row, n_col, node_count),
        in_specs=[vmem] * 2,
        out_specs=[vmem, anywhere, anywhere],
        out_shape=[
            local,
            shape((n_col, blocks, 2 * k_width, TILE), BF16),
            shape((n_row, blocks, 2 * k_width, TILE), BF16),
        ],
        scratch_shapes=[
            pltpu.VMEM((blocks, 2 * k_width, TILE), BF16),
            pltpu.VMEM((n_row, k_width, TILE), F32),
            pltpu.VMEM((n_col, k_width, TILE), F32),
            row_sems, col_sems, row_sems, col_sems, row_sems, col_sems,
            pltpu.SemaphoreType.DMA((2,)),
        ],
        compiler_params=params(0),
    )(block_x, block_p)

    def spread(v, n):
        return v.reshape(n * blocks, v.shape[2], TILE)

    xr, xc, pr, pc = apply_graph(
        slot_rows, slot_cols, count, spread(vrow, n_col), spread(vcol, n_row), vals,
        ((k_width, X_WIRE), (k_width, R_WIRE)),
    )

    residual, image_x, image_p, vrow, vcol = pl.pallas_call(
        functools.partial(middle_kernel, n_row, n_col, node_count),
        in_specs=[vmem] + [anywhere] * 4,
        out_specs=[vmem, vmem, vmem, anywhere, anywhere],
        out_shape=[
            local, local, local,
            shape((n_col, blocks, k_width, TILE), BF16),
            shape((n_row, blocks, k_width, TILE), BF16),
        ],
        scratch_shapes=[
            pltpu.VMEM((n_col, blocks, k_width, TILE), X_WIRE),
            pltpu.VMEM((n_row, blocks, k_width, TILE), X_WIRE),
            pltpu.VMEM((n_col, blocks, k_width, TILE), R_WIRE),
            pltpu.VMEM((n_row, blocks, k_width, TILE), R_WIRE),
            pltpu.VMEM((blocks, k_width, TILE), BF16),
            pltpu.VMEM((n_row, k_width, TILE), F32),
            pltpu.VMEM((n_col, k_width, TILE), F32),
            row_sems, col_sems, row_sems, col_sems, row_sems, col_sems, row_sems, col_sems,
            pltpu.SemaphoreType.DMA((3, 2)),
        ],
        compiler_params=params(1),
    )(ortho, xr, xc, pr, pc)

    rr, rc = apply_graph(
        slot_rows, slot_cols, count, spread(vrow, n_col), spread(vcol, n_row), vals,
        ((k_width, R_WIRE),),
    )

    full = 3 * k_width
    image_r, gram_a, gram_b = pl.pallas_call(
        functools.partial(last_kernel, n_row, n_col, node_count),
        in_specs=[vmem] * 5 + [anywhere] * 2,
        out_specs=[vmem] * 3,
        out_shape=[local, shape((full, full), F32), shape((full, full), F32)],
        scratch_shapes=[
            pltpu.VMEM((n_col, blocks, k_width, TILE), R_WIRE),
            pltpu.VMEM((n_row, blocks, k_width, TILE), R_WIRE),
            pltpu.VMEM((full, 2 * full), F32),
            pltpu.VMEM((full, 2 * full), F32),
            pltpu.VMEM((n_row, full // n_row, 2 * full), F32),
            pltpu.VMEM((n_col, full // n_row, 2 * full), F32),
            row_sems, col_sems, row_sems, col_sems, row_sems,
            pltpu.SemaphoreType.DMA((2,)),
        ],
        compiler_params=params(2),
    )(ortho, residual, block_p, image_x, image_p, rr, rc)
    return residual, image_r, gram_a, gram_b


def solution(mesh):
    in_specs = (
        P(None, ("row", "col")),
        P(None, ("row", "col")),
        P("row", "col", None),
        P("row", "col", None),
        P("row", "col"),
        P("row", "col", None, None, None),
    )
    out_specs = (P(None, ("row", "col")), P(None, ("row", "col")), P(), P())
    return jax.shard_map(
        per_device, mesh=mesh, in_specs=in_specs, out_specs=out_specs, check_vma=False
    )
```

time: 1310 us -> 291 us (0.22)
  waiting for transfers between devices: 591 us -> 0 us
  other arithmetic: 309 us -> 2.57 us
  Pallas kernels: 0 us -> 281 us
  blocking collectives: 149 us -> 0 us
  matrix products: 118 us -> 0 us
  local copies, waits for them, and re-layouts: 118 us -> 5.53 us
  between operations: 15 us -> 1.31 us
    reduce_scatter x4 -> x0, waiting for transfers between devices: 351 us -> none  [the longest x2 186 us: apply_graph(): lax.psum_scatter(col_totals.reshape(vec_width, -1), 'row', scatter_dimens...]
    scatter-add x28 -> x0, other arithmetic: 283 us -> none  [the longest x14 158 us: turn(): row_totals.at[:, row_index].add(forward)]
    pallas_call x0 -> x5, Pallas kernels: none -> 281 us  [the longest x1 116 us: per_device(): pl.pallas_call(functools.partial(middle_kernel, n_row, n_col, node_count)...]
    psum x1 -> x0, waiting for transfers between devices: 148 us -> none  [per_device(): lax.psum((product(basis, images), product(basis, basis)), ('row', 'col'))]
    psum x2 -> x0, blocking collectives: 135 us -> none  [the longest x1 68.9 us: per_device(): gram_x = lax.psum(product(block_x, block_x), ('row', 'col'))]
    dot_general x33 -> x0, matrix products: 118 us -> none  [the longest x14 62.8 us: turn(): jnp.einsum('wgb,gab->wga', col_inputs, values, preferred_element_type=jnp...]
    all_gather x3 -> x0, waiting for transfers between devices: 91.2 us -> none  [the longest x2 71.4 us: apply_graph(): row_range = lax.all_gather(vectors, 'col', axis=1, tiled=True)]
    gather x28 -> x0, local copies, waits for them, and re-layouts: 81.3 us -> none  [the longest x14 43.3 us: turn(): row_inputs = jnp.take(row_blocks, row_index, axis=1)]
  transfers between devices with their start and end apart: 8 -> 0, of which waited for: 8 -> 0; matrix products, arithmetic and copies ran while one was open for 1% -> 0% of each run, Pallas kernels for 0% -> 0%
where the time goes in v1:
time: 291 us; the launch traced here: 290 us
  Pallas kernels  281 us (97%)
  local copies, waits for them, and re-layouts  5.53 us (2%)
    pallas_call x1, Pallas kernels, per_device(): pl.pallas_call(functools.partial(middle_kernel, n_row, n_col, node_count)...  116 us
    pallas_call x1, Pallas kernels, per_device(): pl.pallas_call(functools.partial(first_kernel, n_row, n_col, node_count),...  65.8 us
    pallas_call x1, Pallas kernels, per_device(): pl.pallas_call(functools.partial(last_kernel, n_row, n_col, node_count),...  52.4 us
    pallas_call x2, Pallas kernels, apply_graph(): pl.pallas_call(functools.partial(apply_kernel, [w for w, _ in splits]), g...  46.2 us

profile of v1, /device:TPU:1, one launch (start us, length us, event | category | flops | bytes accessed | tf_op | source)
XLA Modules:
  0.0 290.2 jit_solution(12513334686040591884)
XLA Ops:
  1.3 1.3 reduce.rows_ref
  2.6 1.3 reduce.1.cols_ref
  3.9 65.8 %shard_map.93 = (f32[64,768]{1,0:T(8,128)}, bf16[16,6,128,128]{3,2,1,0:T(8,128)(2,1)}, bf16[8,6,128,128]{3,2,1,0:T(8,128)(2,1)}) custom-call(f32[64,768]{1,0:T(8,128)} %x_ref.1, f32[64,768]{1,0:T(8,128)} %p_ref.3), custom_call_target="tpu_custom_call" | custom-call | tf_op jit(solution)/shard_map/pallas_call | solution.py:419
  69.6 24.8 %shard_map.94 = (f32[96,64,128]{2,1,0:T(8,128)}, f32[48,64,128]{2,1,0:T(8,128)}, bf16[96,64,128]{2,1,0:T(8,128)(2,1)}, bf16[48,64,128]{2,1,0:T(8,128)(2,1)}) custom-call(s32[576]{0:T(1024)} %reduce.rows_ref, s32[576]{0:T(1024)} %reduce.1.cols_ref, s32[1]{0:T(128)} %bitcast.6.count_ref, bf16[96,128,128]{2,1,0:T(8,128)(2,1)} %bitcast.10, ...), custom_call_target="tpu_custom_call" | custom-call | flops 4831838208 | bytes 18874368 | tf_op jit(solution)/shard_map/pallas_call | solution.py:254
  94.5 116.4 %shard_map.95 = (f32[64,768]{1,0:T(8,128)}, f32[64,768]{1,0:T(8,128)}, f32[64,768]{1,0:T(8,128)}, bf16[16,6,64,128]{3,2,1,0:T(8,128)(2,1)}, bf16[8,6,64,128]{3,2,1,0:T(8,128)(2,1)}) custom-call(f32[64,768]{1,0:T(8,128)} %get-tuple-element.21.ortho_ref, f32[96,64,128]{2,1,0:T(8,128)} %get-tuple-element.24.xr_ref, f32[48,64,128]{2,1,0:T(8,128)} %get-tuple-element.25.xc_ref, ...), custom_call_target="tpu_custom_call" | custom-call | tf_op jit(solution)/shard_map/pallas_call | solution.py:446
  210.9 21.4 %shard_map.96 = (bf16[96,64,128]{2,1,0:T(8,128)(2,1)}, bf16[48,64,128]{2,1,0:T(8,128)(2,1)}) custom-call(s32[576]{0:T(1024)} %reduce.rows_ref, s32[576]{0:T(1024)} %reduce.1.cols_ref, s32[1]{0:T(128)} %bitcast.7.count_ref, bf16[96,64,128]{2,1,0:T(8,128)(2,1)} %bitcast.11, bf16[48,64,128]{2,1,0:T(8,128)(2,1)} %bitcast.13, bf16[576,128,128]{2,1,0:T(8,128)(2,1)} %bitcast.9), custom_call_target="tpu_custom_call" | custom-call | flops 2415919104 | bytes 18874368 | tf_op jit(solution)/shard_map/pallas_call | solution.py:254
  232.3 0.0 copy-start
  232.3 52.4 %shard_map.97 = (f32[64,768]{1,0:T(8,128)}, f32[192,192]{1,0:T(8,128)}, f32[192,192]{1,0:T(8,128)}) custom-call(f32[64,768]{1,0:T(8,128)} %get-tuple-element.21.ortho_ref, f32[64,768]{1,0:T(8,128)} %get-tuple-element.42.residual_ref, f32[64,768]{1,0:T(8,128)} %p_ref.3, f32[64,768]{1,0:T(8,128)} %get-tuple-element.29.image_x_ref, ...), custom_call_target="tpu_custom_call" | custom-call | tf_op jit(solution)/shard_map/pallas_call | solution.py:475
  284.6 0.0 copy-done
  284.6 0.7 copy.15
  285.3 1.6 copy.16
  286.9 1.6 copy.17
  288.6 1.6 copy.18
Async XLA Ops:
  232.3 52.4 %copy-start = (f32[64,768]{1,0:T(8,128)S(1)}, f32[64,768]{1,0:T(8,128)}, u32[]{:S(2)}) copy-start(f32[64,768]{1,0:T(8,128)} %get-tuple-element.42.residual_ref) | copy-start | bytes 589828

commit v2 on v1

v2 whole, which is shorter than its diff:
```python
import functools

import jax
import jax.numpy as jnp
from jax import lax
from jax.experimental import pallas as pl
from jax.experimental.pallas import tpu as pltpu
from jax.sharding import PartitionSpec as P

F32 = jnp.float32
BF16 = jnp.bfloat16
TILE = 128
HIGHEST = lax.Precision.HIGHEST
MESH = pl.DeviceIdType.MESH
VMEM_LIMIT = 56 * 2**20
GROUP = 48
SIDE = 4
HALF = 3
SPARE = 16
TOP = 32700.0


def dot_nt(left, right):
    return lax.dot_general(
        left, right, (((1,), (1,)), ((), ())), precision=HIGHEST, preferred_element_type=F32
    )


def dot_tn(left, right):
    return lax.dot_general(
        left, right, (((0,), (0,)), ((), ())), precision=HIGHEST, preferred_element_type=F32
    )


def dot_nn(left, right):
    return lax.dot_general(
        left, right, (((1,), (0,)), ((), ())), precision=HIGHEST, preferred_element_type=F32
    )


class Line:
    def __init__(self, name, size):
        self.name, self.size = name, size
        self.me = lax.axis_index(name)

    def ahead(self, k):
        return lax.rem(self.me + k, self.size)

    def behind(self, k):
        return lax.rem(self.me + self.size - k, self.size)

    def greet(self, barrier):
        for k in range(1, self.size):
            pl.semaphore_signal(
                barrier, inc=1, device_id={self.name: self.ahead(k)}, device_id_type=MESH
            )

    def copies(self, source, target, send_sem, recv_sem):
        return [
            pltpu.make_async_remote_copy(
                src_ref=source(self.ahead(k)),
                dst_ref=target(self.me),
                send_sem=send_sem.at[k],
                recv_sem=recv_sem.at[k],
                device_id={self.name: self.ahead(k)},
                device_id_type=MESH,
            )
            for k in range(1, self.size)
        ]

    def arrivals(self, source, target, send_sem, recv_sem):
        return [
            pltpu.make_async_remote_copy(
                src_ref=source(self.ahead(k)),
                dst_ref=target(self.behind(k)),
                send_sem=send_sem.at[k],
                recv_sem=recv_sem.at[k],
                device_id={self.name: self.ahead(k)},
                device_id_type=MESH,
            )
            for k in range(1, self.size)
        ]


class Exchange:
    def __init__(self, line, source, target, sems):
        self.sent = line.copies(source, target, sems.at[0], sems.at[1])
        self.come = line.arrivals(source, target, sems.at[0], sems.at[1])

    def start(self):
        for c in self.sent:
            c.start()
        return self

    def wait_recv(self):
        for c in self.come:
            c.wait_recv()
        return self

    def wait_send(self):
        for c in self.sent:
            c.wait_send()
        return self


def pack(parts, ref):
    width = parts[0].shape[0]
    most = jnp.abs(parts[0])
    for part in parts[1:]:
        most = jnp.maximum(most, jnp.abs(part))
    most = jnp.maximum(jnp.max(most, axis=1, keepdims=True), 1e-30)
    power = jnp.clip(jnp.ceil(jnp.log2(most)), -100.0, 126.0)
    up = jnp.exp2(-power) * TOP
    for i, part in enumerate(parts):
        ref[i * width : (i + 1) * width, :] = jnp.round(part * up).astype(jnp.int32).astype(jnp.int16)
    down = lax.broadcasted_iota(jnp.int32, (width, TILE), 0)
    across = lax.broadcasted_iota(jnp.int32, (width, TILE), 1)
    line = jnp.sum(jnp.where(down == across, power, 0.0), axis=0, keepdims=True)
    line = jnp.broadcast_to(line, (SPARE, TILE))
    ref[len(parts) * width :, :] = line.astype(jnp.int32).astype(jnp.int16)


def unpack(ref, count, width):
    line = ref[count * width :, :].astype(jnp.int32).astype(F32)[:1]
    down = lax.broadcasted_iota(jnp.int32, (width, TILE), 0)
    across = lax.broadcasted_iota(jnp.int32, (width, TILE), 1)
    power = jnp.sum(jnp.where(down == across, line, 0.0), axis=1, keepdims=True)
    step = jnp.exp2(power) * (1.0 / TOP)
    return [
        ref[i * width : (i + 1) * width, :].astype(jnp.int32).astype(F32) * step
        for i in range(count)
    ]


def add_lists(lists):
    return [functools.reduce(lambda a, b: a + b, parts) for parts in zip(*lists)]


class Plane:
    def __init__(self, cols):
        self.spot = (cols.me // SIDE, lax.rem(cols.me, SIDE))

    def axes(self, half):
        return (self.spot[0], self.spot[1]) if half == 0 else (self.spot[1], self.spot[0])

    def index(self, half, first, second):
        first, second = lax.rem(first, SIDE), lax.rem(second, SIDE)
        return first * SIDE + second if half == 0 else second * SIDE + first

    def copy(self, source, target, sems, at, device):
        return pltpu.make_async_remote_copy(
            src_ref=source,
            dst_ref=target,
            send_sem=sems.at[(0, *at)],
            recv_sem=sems.at[(1, *at)],
            device_id={"col": device},
            device_id_type=MESH,
        )


class PlaneGather:
    def __init__(self, plane, mine, slot, sems):
        self.plane, self.mine, self.slot, self.sems = plane, mine, slot, sems
        self.sent = []

    def send(self, source, owner, half, at, device):
        c = self.plane.copy(source, self.slot(owner, half), self.sems, at, device)
        c.start()
        self.sent.append(c)

    def arrived(self, owner, half, at):
        _, device = self.place(half, 1, 0)
        self.plane.copy(self.mine(half), self.slot(owner, half), self.sems, at, device).wait_recv()

    def place(self, half, first, second):
        f, s = self.plane.axes(half)
        return (
            self.plane.index(half, f + SIDE - first, s + SIDE - second),
            self.plane.index(half, f + first, s + second),
        )

    def start(self):
        for half in (0, 1):
            me, _ = self.place(half, 0, 0)
            for k in range(1, SIDE):
                self.send(self.mine(half), me, half, (half, k, 0), self.place(half, k, 0)[1])
        for half in (0, 1):
            me, _ = self.place(half, 0, 0)
            for k in range(1, SIDE):
                self.send(self.mine(half), me, half, (half, 0, k), self.place(half, 0, k)[1])

    def forward(self):
        for i in (1, 3, 2):
            for half in (0, 1):
                owner, _ = self.place(half, i, 0)
                self.arrived(owner, half, (half, i, 0))
                for k in range(1, SIDE):
                    self.send(
                        self.slot(owner, half), owner, half, (half, i, k), self.place(half, 0, k)[1]
                    )

    def wait_recv(self):
        for i in range(SIDE):
            for k in range(1, SIDE):
                for half in (0, 1):
                    self.arrived(self.place(half, i, k)[0], half, (half, i, k))

    def wait_send(self):
        for c in self.sent:
            c.wait_send()


class PlaneSum:
    def __init__(self, plane, packed, first_in, second_in, second_out, sems1, sems2, own):
        self.plane, self.packed = plane, packed
        self.first_in, self.second_in, self.second_out = first_in, second_in, second_out
        self.sems1, self.sems2 = sems1, sems2
        self.own = [
            pltpu.make_async_copy(
                packed.at[h, pl.ds(plane.axes(h)[0] * SIDE, SIDE)], first_in.at[h, 0], own.at[h]
            )
            for h in (0, 1)
        ]
        self.sent = []

    def hop(self, half, k, j):
        f, s = self.plane.axes(half)
        return self.plane.copy(
            self.packed.at[half, lax.rem(f + k, SIDE) * SIDE + j],
            self.first_in.at[half, k, j],
            self.sems1,
            (half, k, j),
            self.plane.index(half, f + k, s),
        )

    def hop2(self, half, k):
        f, s = self.plane.axes(half)
        return self.plane.copy(
            self.second_out.at[half, k],
            self.second_in.at[half, k],
            self.sems2,
            (half, k),
            self.plane.index(half, f, s + k),
        )

    def start(self):
        for n in (2, 1, 3, 0):
            for half in (0, 1):
                for k in (2, 1, 3):
                    c = self.hop(half, k, self.turn(half, n))
                    c.start()
                    self.sent.append(c)
        for c in self.own:
            c.start()

    def turn(self, half, n):
        return lax.rem(self.plane.axes(half)[1] + n, SIDE)

    def gathered(self, half, k, width):
        j = self.turn(half, k)
        for i in range(1, SIDE):
            self.hop(half, i, j).wait_recv()
        return add_lists(
            [unpack(self.first_in.at[half, i, j], HALF, width) for i in range(SIDE)]
        )

    def pass_on(self, width):
        for c in self.own:
            c.wait()
        for k in (2, 1, 3):
            for half in (0, 1):
                pack(self.gathered(half, k, width), self.second_out.at[half, k])
                c = self.hop2(half, k)
                c.start()
                self.sent.append(c)

    def finish(self, width):
        mine = [self.gathered(half, 0, width) for half in (0, 1)]
        blocks = []
        for half in (0, 1):
            parts = [mine[half]]
            for k in (2, 1, 3):
                self.hop2(half, k).wait_recv()
                parts.append(unpack(self.second_in.at[half, k], HALF, width))
            blocks += add_lists(parts)
        return blocks

    def wait_send(self):
        for c in self.sent:
            c.wait_send()


class RowSum:
    def __init__(self, rows, packed, inbox, sems, own):
        self.rows, self.inbox = rows, inbox
        self.move = Exchange(rows, lambda p: packed.at[p], lambda s: inbox.at[s], sems)
        self.own = pltpu.make_async_copy(packed.at[rows.me], inbox.at[rows.me], own)

    def start(self):
        self.move.start()
        self.own.start()

    def finish(self, count, width):
        self.own.wait()
        self.move.wait_recv()
        return add_lists([unpack(self.inbox.at[j], count, width) for j in range(self.rows.size)])

    def wait_send(self):
        self.move.wait_send()


def enter(rows, cols):
    barrier = pltpu.get_barrier_semaphore()
    rows.greet(barrier)
    cols.greet(barrier)
    pl.semaphore_wait(barrier, rows.size + cols.size - 2)


def sum_slots(ref, count):
    total = ref[0]
    for j in range(1, count):
        total = total + ref[j]
    return total


def all_reduce(rows, cols, part, first, second, row_sems, col_sems, between=None):
    half = part.shape[0] // 2
    first[rows.me] = jnp.concatenate([part[:half], part[half:]], axis=1)
    one = Exchange(rows, lambda p: first.at[rows.me], lambda s: first.at[s], row_sems)
    one.start().wait_recv()
    second[cols.me] = sum_slots(first, rows.size)
    two = Exchange(cols, lambda p: second.at[cols.me], lambda s: second.at[s], col_sems)
    two.start()
    if between is not None:
        between()
    two.wait_recv()
    total = sum_slots(second, cols.size)
    one.wait_send()
    two.wait_send()
    return jnp.concatenate([total[:, : 2 * half], total[:, 2 * half :]], axis=0)


def factor(gram):
    k_width = gram.shape[0]
    row_id = lax.broadcasted_iota(jnp.int32, (k_width, k_width), 0)
    col_id = lax.broadcasted_iota(jnp.int32, (k_width, k_width), 1)
    eye = jnp.where(row_id == col_id, 1.0, 0.0).astype(F32)
    work = jnp.concatenate([gram, eye], axis=1)
    down = lax.broadcasted_iota(jnp.int32, (k_width, 2 * k_width), 0)
    pivots = []
    for k in range(k_width):
        pivot_row = work[k : k + 1, :]
        pivot = work[k : k + 1, k : k + 1]
        pivots.append(pivot)
        if k + 1 < k_width:
            ratio = work[:, k : k + 1]
            work = work - jnp.where(down > k, ratio * (pivot_row * (1.0 / pivot)), 0.0)
    scale = lax.rsqrt(jnp.concatenate(pivots, axis=0))
    return work[:, k_width:] * scale


def first_kernel(
    n_row, n_col, node_count, x_ref, p_ref, ortho_ref, vrow_ref, vcol_ref,
    low, first, second, ar_row, ar_col, p_row, p_plane, x_row, x_plane, own,
):
    rows, cols = Line("row", n_row), Line("col", n_col)
    plane = Plane(cols)
    k_width, mine = x_ref.shape
    blocks = mine // TILE
    enter(rows, cols)
    for b in range(blocks):
        low[b, k_width:, :] = p_ref[:, b * TILE : (b + 1) * TILE].astype(BF16)
    part = dot_nt(x_ref[...], x_ref[...]) / node_count

    def gathers(band, row_sems, plane_sems):
        across = PlaneGather(
            plane,
            lambda h: low.at[pl.ds(h * HALF, HALF), band, :],
            lambda owner, h: vrow_ref.at[owner, pl.ds(h * HALF, HALF), band, :],
            plane_sems,
        )
        along = Exchange(
            rows, lambda p: low.at[:, band, :], lambda s: vcol_ref.at[s, :, band, :], row_sems
        )
        return across, along

    p_across, p_along = gathers(pl.ds(k_width, k_width), p_row, p_plane)
    x_across, x_along = gathers(pl.ds(0, k_width), x_row, x_plane)

    def give_p():
        p_across.start()
        p_along.start()

    gram = all_reduce(rows, cols, part, first, second, ar_row, ar_col, give_p)
    p_across.forward()
    ortho = dot_nn(factor(gram), x_ref[...])
    ortho_ref[...] = ortho
    for b in range(blocks):
        low[b, :k_width, :] = ortho[:, b * TILE : (b + 1) * TILE].astype(BF16)
    x_across.start()
    x_along.start()
    here = [
        pltpu.make_async_copy(low, vrow_ref.at[cols.me], own.at[0]),
        pltpu.make_async_copy(low, vcol_ref.at[rows.me], own.at[1]),
    ]
    for c in here:
        c.start()
    x_across.forward()
    moves = (p_across, p_along, x_across, x_along)
    for m in moves:
        m.wait_recv()
    for m in moves:
        m.wait_send()
    for c in here:
        c.wait()


def times(left, right, right_dim):
    return lax.dot_general(
        left, right, (((1,), (right_dim,)), ((), ())), preferred_element_type=F32
    )


def apply_kernel(
    k_width, rows_ref, cols_ref, count_ref, vrow_ref, vcol_ref, tile_ref, *rest
):
    n_out = (len(rest) - 8) // 2
    outs, boxes = rest[:n_out], rest[n_out : 2 * n_out]
    vrow, vcol, tiles, row_acc, col_acc, tile_sems, in_sems, out_sems = rest[2 * n_out :]
    row_blocks, width, _ = vrow.shape
    col_blocks = vcol.shape[0]
    count = count_ref[0, 0]
    groups = (count + GROUP - 1) // GROUP

    def tile_copy(g):
        part = pl.ds(g * GROUP, GROUP)
        return pltpu.make_async_copy(tile_ref.at[part], tiles.at[part], tile_sems.at[g])

    def start_copy(g, carry):
        tile_copy(g).start()
        return carry

    inputs = [
        pltpu.make_async_copy(vcol_ref, vcol, in_sems.at[0]),
        pltpu.make_async_copy(vrow_ref, vrow, in_sems.at[1]),
    ]
    tile_copy(0).start()
    for c in inputs:
        c.start()
    lax.fori_loop(1, groups, start_copy, 0)
    row_acc[...] = jnp.zeros_like(row_acc)
    col_acc[...] = jnp.zeros_like(col_acc)
    for c in inputs:
        c.wait()

    def place(slot):
        live = slot < count
        a, b = rows_ref[0, 0, slot], cols_ref[0, 0, slot]
        return a, b, jnp.where(live, a, row_blocks), jnp.where(live, b, col_blocks)

    def single(slot):
        a, b, to_row, to_col = place(slot)
        tile = tiles[slot]
        row_acc[to_row] += times(vcol[b], tile, 1)
        col_acc[to_col] += times(vrow[a], tile, 0)

    def pair(slot):
        a, b, to_row, to_col = place(slot)
        a2, b2, to_row2, to_col2 = place(slot + 1)
        tile, tile2 = tiles[slot], tiles[slot + 1]
        none = jnp.zeros((width, TILE), BF16)

        def beside(u, v):
            return jnp.concatenate(
                [jnp.concatenate([u, none], axis=1), jnp.concatenate([none, v], axis=1)], axis=0
            )

        forward = times(beside(vcol[b], vcol[b2]), jnp.concatenate([tile, tile2], axis=1), 1)
        row_acc[to_row] += forward[:width]
        row_acc[to_row2] += forward[width:]
        backward = times(beside(vrow[a], vrow[a2]), jnp.concatenate([tile, tile2], axis=0), 0)
        col_acc[to_col] += backward[:width]
        col_acc[to_col2] += backward[width:]

    def group(g, carry):
        tile_copy(g).wait()
        if width < TILE:
            for u in range(0, GROUP, 2):
                pair(g * GROUP + u)
        else:
            for u in range(GROUP):
                single(g * GROUP + u)
        return carry

    lax.fori_loop(0, groups, group, 0)

    row_box, col_box = boxes[:2]
    n_row, n_col = col_box.shape[0], row_box.shape[1]
    blocks = row_blocks // n_col

    def pack_row(c, carry):
        for half in (0, 1):
            at = c if half == 0 else lax.rem(c, SIDE) * SIDE + c // SIDE
            parts = [row_acc[c * blocks + half * HALF + i, :k_width, :] for i in range(HALF)]
            pack(parts, row_box.at[half, at])
        return carry

    def pack_col(r, carry):
        pack([col_acc[r * blocks + i, :k_width, :] for i in range(blocks)], col_box.at[r])
        return carry

    results = [
        pltpu.make_async_copy(box, out, out_sems.at[i]) for i, (box, out) in enumerate(zip(boxes, outs))
    ]
    lax.fori_loop(0, n_col, pack_row, 0)
    results[0].start()
    lax.fori_loop(0, n_row, pack_col, 0)
    results[1].start()
    for i in range(2, n_out):
        acc, n = ((row_acc, row_blocks), (col_acc, col_blocks))[i - 2]
        boxes[i][...] = acc[:n, k_width:, :].astype(boxes[i].dtype)
        results[i].start()
    for c in results:
        c.wait()


def apply_graph(tile_rows, tile_cols, count, vrow, vcol, vals, k_width):
    n_col, blocks, width, _ = vrow.shape
    n_row = vcol.shape[0]
    slots = vals.shape[0]
    row_blocks, col_blocks = n_col * blocks, n_row * blocks
    smem = pl.BlockSpec(memory_space=pltpu.SMEM)
    anywhere = pl.BlockSpec(memory_space=pl.ANY)
    shape = jax.ShapeDtypeStruct
    out_shape = [
        shape((2, n_col, HALF * k_width + SPARE, TILE), jnp.int16),
        shape((n_row, blocks * k_width + SPARE, TILE), jnp.int16),
    ]
    if width > k_width:
        out_shape += [shape((n, width - k_width, TILE), BF16) for n in (row_blocks, col_blocks)]
    return pl.pallas_call(
        functools.partial(apply_kernel, k_width),
        in_specs=[smem] * 3 + [anywhere] * 3,
        out_specs=[anywhere] * len(out_shape),
        out_shape=out_shape,
        scratch_shapes=[
            *[pltpu.VMEM(o.shape, o.dtype) for o in out_shape],
            pltpu.VMEM((row_blocks, width, TILE), BF16),
            pltpu.VMEM((col_blocks, width, TILE), BF16),
            pltpu.VMEM((slots, TILE, TILE), BF16),
            pltpu.VMEM((row_blocks + 1, width, TILE), F32),
            pltpu.VMEM((col_blocks + 1, width, TILE), F32),
            pltpu.SemaphoreType.DMA((slots // GROUP,)),
            pltpu.SemaphoreType.DMA((2,)),
            pltpu.SemaphoreType.DMA((len(out_shape),)),
        ],
        compiler_params=pltpu.CompilerParams(vmem_limit_bytes=VMEM_LIMIT),
        cost_estimate=pl.CostEstimate(
            flops=16 * slots * width * TILE * TILE,
            bytes_accessed=2 * slots * TILE * TILE,
            transcendentals=0,
        ),
    )(
        tile_rows, tile_cols, count,
        vrow.reshape(row_blocks, width, TILE), vcol.reshape(col_blocks, width, TILE), vals,
    )


def middle_kernel(
    n_row, n_col, node_count, ortho_ref, xr_ref, xc_ref, pc_ref,
    residual_ref, image_x_ref, vrow_ref, vcol_ref, p_box_ref,
    first_in, second_in, second_out, inbox, low, first, second,
    s1, s2, s_row, ar_row, ar_col, g_row, g_plane, p_row, own,
):
    rows, cols = Line("row", n_row), Line("col", n_col)
    plane = Plane(cols)
    k_width, mine = ortho_ref.shape
    blocks = mine // TILE
    enter(rows, cols)
    across = PlaneSum(plane, xr_ref, first_in, second_in, second_out, s1, s2, own)
    along = RowSum(rows, xc_ref, inbox, s_row, own.at[2])
    across.start()
    along.start()
    across.pass_on(k_width)
    from_rows = along.finish(blocks, k_width)
    images = add_lists([across.finish(k_width), from_rows])
    image = jnp.concatenate(images, axis=1)
    image_x_ref[...] = image
    ortho = ortho_ref[...]
    part = dot_nt(ortho, image) / node_count
    p_along = Exchange(rows, lambda p: pc_ref.at[p], lambda s: p_box_ref.at[s], p_row)
    rayleigh = all_reduce(rows, cols, part, first, second, ar_row, ar_col, p_along.start)
    residual = image_x_ref[...] - dot_tn(rayleigh, ortho)
    residual_ref[...] = residual
    for b in range(blocks):
        low[b] = residual[:, b * TILE : (b + 1) * TILE].astype(BF16)
    g_across = PlaneGather(
        plane,
        lambda h: low.at[pl.ds(h * HALF, HALF)],
        lambda owner, h: vrow_ref.at[owner, pl.ds(h * HALF, HALF)],
        g_plane,
    )
    g_along = Exchange(rows, lambda p: low, lambda s: vcol_ref.at[s], g_row)
    g_across.start()
    g_along.start()
    here = [
        pltpu.make_async_copy(low, vrow_ref.at[cols.me], own.at[3]),
        pltpu.make_async_copy(low, vcol_ref.at[rows.me], own.at[4]),
        pltpu.make_async_copy(pc_ref.at[rows.me], p_box_ref.at[rows.me], own.at[5]),
    ]
    for c in here:
        c.start()
    g_across.forward()
    g_across.wait_recv()
    g_along.wait_recv()
    p_along.wait_recv()
    for c in here:
        c.wait()
    for c in (across, along, g_across, g_along, p_along):
        c.wait_send()


class Spread:
    def __init__(self, rows, cols, whole, first, second, done, sems):
        share = whole.shape[0] // rows.size
        mine = lambda p: pl.ds(pl.multiple_of(p * share, 8), share)
        one, two, three = sems
        self.rows, self.cols, self.mine = rows, cols, mine
        self.whole, self.first, self.second, self.done = whole, first, second, done
        self.one = Exchange(rows, lambda p: whole.at[mine(p)], lambda s: first.at[s], one)
        self.two = Exchange(cols, lambda p: second.at[cols.me], lambda s: second.at[s], two)
        self.three = Exchange(
            rows, lambda p: done.at[mine(rows.me)], lambda s: done.at[mine(s)], three
        )

    def start(self):
        self.first[self.rows.me] = self.whole[self.mine(self.rows.me), :]
        self.one.start()

    def turn(self):
        self.one.wait_recv()
        self.second[self.cols.me] = sum_slots(self.first, self.rows.size)
        self.two.start()

    def back(self):
        self.two.wait_recv()
        self.done[self.mine(self.rows.me), :] = sum_slots(self.second, self.cols.size)
        self.three.start()

    def finish(self):
        self.three.wait_recv()
        for e in (self.one, self.two, self.three):
            e.wait_send()


def last_kernel(
    n_row, n_col, node_count, ortho_ref, residual_ref, p_ref, image_x_ref, pr_ref, pc_ref,
    rr_ref, rc_ref, image_r_ref, early_ref, late_ref,
    first_in, second_in, second_out, inbox,
    e_whole, e_first, e_second, e_done, l_whole, l_first, l_second, l_done,
    s1, s2, s_row, e1, e2, e3, l1, l2, l3, own,
):
    rows, cols = Line("row", n_row), Line("col", n_col)
    plane = Plane(cols)
    k_width, mine = ortho_ref.shape
    blocks = mine // TILE
    enter(rows, cols)
    across = PlaneSum(plane, rr_ref, first_in, second_in, second_out, s1, s2, own)
    along = RowSum(rows, rc_ref, inbox, s_row, own.at[2])
    across.start()
    along.start()
    basis = jnp.concatenate([ortho_ref[...], residual_ref[...], p_ref[...]], axis=0)
    image_p = []
    for b in range(blocks):
        total = pr_ref[0, b].astype(F32)
        for j in range(1, n_col):
            total = total + pr_ref[j, b].astype(F32)
        for j in range(n_row):
            total = total + pc_ref[j, b].astype(F32)
        image_p.append(total)
    others = jnp.concatenate([image_x_ref[...], jnp.concatenate(image_p, axis=1)], axis=0)
    e_whole[:, : 2 * k_width] = dot_nt(basis, others) / node_count
    gram_b = dot_nt(basis, basis) / node_count
    pad = jnp.zeros((3 * k_width, k_width), F32)
    e_whole[:, 2 * k_width :] = jnp.concatenate([gram_b, pad], axis=1)
    early = Spread(rows, cols, e_whole, e_first, e_second, e_done, (e1, e2, e3))
    late = Spread(rows, cols, l_whole, l_first, l_second, l_done, (l1, l2, l3))
    early.start()
    across.pass_on(k_width)
    early.turn()
    from_rows = along.finish(blocks, k_width)
    images = add_lists([across.finish(k_width), from_rows])
    image_r = jnp.concatenate(images, axis=1)
    image_r_ref[...] = image_r
    l_whole[...] = jnp.concatenate([dot_nt(basis, image_r) / node_count, pad], axis=1)
    late.start()
    early.back()
    late.turn()
    late.back()
    early.finish()
    early_ref[...] = e_done[...]
    late.finish()
    late_ref[...] = l_done[...]
    across.wait_send()
    along.wait_send()


def hand_kernel(residual_in, image_in, early_ref, late_ref, residual_ref, image_ref, a_ref, b_ref):
    residual_ref[...] = residual_in[...]
    image_ref[...] = image_in[...]
    k_width = residual_in.shape[0]
    x_cols, p_cols = early_ref[:, :k_width], early_ref[:, k_width : 2 * k_width]
    a_ref[...] = jnp.concatenate([x_cols, late_ref[:, :k_width], p_cols], axis=1)
    b_ref[...] = early_ref[:, 2 * k_width : 5 * k_width]


def per_device(block_x, block_p, tile_rows, tile_cols, tile_count, tile_vals):
    n_row, n_col = lax.axis_size("row"), lax.axis_size("col")
    k_width, mine = block_x.shape
    node_count = mine * n_row * n_col
    blocks = mine // TILE
    slots = tile_vals.shape[2]
    vals = tile_vals.reshape(slots, TILE, TILE)
    vmem = pl.BlockSpec(memory_space=pltpu.VMEM)
    anywhere = pl.BlockSpec(memory_space=pl.ANY)
    row_sems = pltpu.SemaphoreType.DMA((2, n_row))
    col_sems = pltpu.SemaphoreType.DMA((2, n_col))
    plane_sems = pltpu.SemaphoreType.DMA((2, 2, SIDE, SIDE))
    ring_sems = pltpu.SemaphoreType.DMA((2, 2, SIDE))
    shape = jax.ShapeDtypeStruct
    params = lambda i: pltpu.CompilerParams(
        collective_id=i, has_side_effects=True, vmem_limit_bytes=VMEM_LIMIT
    )
    local = shape((k_width, mine), F32)
    half_rows, all_rows = HALF * k_width + SPARE, blocks * k_width + SPARE
    sum_boxes = [
        pltpu.VMEM((2, SIDE, SIDE, half_rows, TILE), jnp.int16),
        pltpu.VMEM((2, SIDE, half_rows, TILE), jnp.int16),
        pltpu.VMEM((2, SIDE, half_rows, TILE), jnp.int16),
        pltpu.VMEM((n_row, all_rows, TILE), jnp.int16),
    ]
    small = [
        pltpu.VMEM((n_row, k_width // 2, 2 * k_width), F32),
        pltpu.VMEM((n_col, k_width // 2, 2 * k_width), F32),
    ]

    ortho, vrow, vcol = pl.pallas_call(
        functools.partial(first_kernel, n_row, n_col, node_count),
        in_specs=[vmem] * 2,
        out_specs=[vmem, anywhere, anywhere],
        out_shape=[
            local,
            shape((n_col, blocks, 2 * k_width, TILE), BF16),
            shape((n_row, blocks, 2 * k_width, TILE), BF16),
        ],
        scratch_shapes=[
            pltpu.VMEM((blocks, 2 * k_width, TILE), BF16),
            *small,
            row_sems, col_sems, row_sems, plane_sems, row_sems, plane_sems,
            pltpu.SemaphoreType.DMA((2,)),
        ],
        compiler_params=params(0),
    )(block_x, block_p)

    xr, xc, pr, pc = apply_graph(tile_rows, tile_cols, tile_count, vrow, vcol, vals, k_width)
    pc = pc.reshape(n_row, blocks, k_width, TILE)

    residual, image_x, vrow, vcol, pc = pl.pallas_call(
        functools.partial(middle_kernel, n_row, n_col, node_count),
        in_specs=[vmem] + [anywhere] * 3,
        out_specs=[vmem, vmem] + [anywhere] * 3,
        out_shape=[
            local, local,
            shape((n_col, blocks, k_width, TILE), BF16),
            shape((n_row, blocks, k_width, TILE), BF16),
            shape((n_row, blocks, k_width, TILE), BF16),
        ],
        scratch_shapes=[
            *sum_boxes,
            pltpu.VMEM((blocks, k_width, TILE), BF16),
            *small,
            plane_sems, ring_sems, row_sems, row_sems, col_sems, row_sems, plane_sems, row_sems,
            pltpu.SemaphoreType.DMA((6,)),
        ],
        compiler_params=params(1),
    )(ortho, xr, xc, pc)

    pr, vcol = lax.optimization_barrier((pr, vcol))
    pr = lax.all_to_all(
        pr.reshape(n_col, blocks, k_width, TILE), "col", split_axis=0, concat_axis=0, tiled=True
    )

    rr, rc = apply_graph(tile_rows, tile_cols, tile_count, vrow, vcol, vals, k_width)

    full = 3 * k_width
    spread = lambda width: [
        pltpu.VMEM((full, width), F32),
        pltpu.VMEM((n_row, full // n_row, width), F32),
        pltpu.VMEM((n_col, full // n_row, width), F32),
        pltpu.VMEM((full, width), F32),
    ]
    image_r, early, late = pl.pallas_call(
        functools.partial(last_kernel, n_row, n_col, node_count),
        in_specs=[vmem] * 6 + [anywhere] * 2,
        out_specs=[vmem] * 3,
        out_shape=[local, shape((full, 6 * k_width), F32), shape((full, 2 * k_width), F32)],
        scratch_shapes=[
            *sum_boxes, *spread(6 * k_width), *spread(2 * k_width),
            plane_sems, ring_sems, row_sems,
            row_sems, col_sems, row_sems, row_sems, col_sems, row_sems,
            pltpu.SemaphoreType.DMA((3,)),
        ],
        compiler_params=params(2),
    )(ortho, residual, block_p, image_x, pr, pc, rr, rc)
    return tuple(
        pl.pallas_call(
            hand_kernel,
            in_specs=[vmem] * 4,
            out_specs=[vmem] * 4,
            out_shape=[local, local, shape((full, full), F32), shape((full, full), F32)],
        )(residual, image_r, early, late)
    )


def solution(mesh):
    in_specs = (
        P(None, ("row", "col")),
        P(None, ("row", "col")),
        P("row", "col", None),
        P("row", "col", None),
        P("row", "col"),
        P("row", "col", None, None, None),
    )
    out_specs = (P(None, ("row", "col")), P(None, ("row", "col")), P(), P())
    return jax.shard_map(
        per_device, mesh=mesh, in_specs=in_specs, out_specs=out_specs, check_vma=False
    )
```

time: 291 us -> 193 us (0.66)
  Pallas kernels: 281 us -> 176 us
  waiting for transfers between devices: 0 us -> 9.67 us
  starting transfers between devices: 0 us -> 4.99 us
  local copies, waits for them, and re-layouts: 5.53 us -> 1.13 us
    pallas_call x1, Pallas kernels: 116 us -> 47.6 us  [per_device(): pl.pallas_call(functools.partial(middle_kernel, n_row, n_col, node_count)...]
    pallas_call x1, Pallas kernels: 65.8 us -> 44.5 us  [per_device(): pl.pallas_call(functools.partial(first_kernel, n_row, n_col, node_count),...]
    pallas_call x1, Pallas kernels: 52.4 us -> 41 us  [per_device(): pl.pallas_call(functools.partial(last_kernel, n_row, n_col, node_count),...]
    all_to_all x0 -> x1, waiting for transfers between devices: none -> 9.67 us  [per_device(): lax.all_to_all(pr.reshape(n_col, blocks, k_width, TILE), 'col', split_axi...]
    all_to_all x0 -> x1, starting transfers between devices: none -> 4.99 us  [per_device(): lax.all_to_all(pr.reshape(n_col, blocks, k_width, TILE), 'col', split_axi...]
    unnamed x6 -> x2, local copies, waits for them, and re-layouts: 5.53 us -> 1.13 us
    pallas_call x2 -> x3, Pallas kernels: 46.2 us -> 42.5 us  [the longest x2 40.4 us: apply_graph(): pl.pallas_call(functools.partial(apply_kernel, k_width), in_specs=[smem]...]
  transfers between devices with their start and end apart: 0 -> 1, of which waited for: 0 -> 1; matrix products, arithmetic and copies ran while one was open for 0% -> 0% of each run, Pallas kernels for 0% -> 9%
where the time goes in v2:
time: 193 us
  Pallas kernels  176 us (91%)
  waiting for transfers between devices  9.67 us (5%)
  starting transfers between devices  4.99 us (3%)
    pallas_call x1, Pallas kernels, per_device(): pl.pallas_call(functools.partial(middle_kernel, n_row, n_col, node_count)...  47.6 us
    pallas_call x1, Pallas kernels, per_device(): pl.pallas_call(functools.partial(first_kernel, n_row, n_col, node_count),...  44.5 us
    pallas_call x1, Pallas kernels, per_device(): pl.pallas_call(functools.partial(last_kernel, n_row, n_col, node_count),...  41 us
    pallas_call x2, Pallas kernels, apply_graph(): pl.pallas_call(functools.partial(apply_kernel, k_width), in_specs=[smem]...  40.4 us
    all_to_all x1, waiting for transfers between devices, per_device(): lax.all_to_all(pr.reshape(n_col, blocks, k_width, TILE), 'col', split_axi...  9.67 us
    all_to_all x1, starting transfers between devices, per_device(): lax.all_to_all(pr.reshape(n_col, blocks, k_width, TILE), 'col', split_axi...  4.99 us
  transfers between devices with their start and end apart: 1, of which 1 were waited for; matrix products, arithmetic and copies ran while one was open for 0% of the time, Pallas kernels for 9%

profile of v2, /device:TPU:1, one launch (start us, length us, event | category | flops | bytes accessed | tf_op | source)
XLA Modules:
  0.0 192.7 jit_solution(8078341023951361903)
XLA Ops:
  1.3 44.5 %shard_map.93 = (f32[64,768]{1,0:T(8,128)}, bf16[16,6,128,128]{3,2,1,0:T(8,128)(2,1)}, bf16[8,6,128,128]{3,2,1,0:T(8,128)(2,1)}) custom-call(f32[64,768]{1,0:T(8,128)} %x_ref.1, f32[64,768]{1,0:T(8,128)} %p_ref.3), custom_call_target="tpu_custom_call" | custom-call | tf_op jit(solution)/shard_map/pallas_call | solution.py:747
  45.7 23.3 %shard_map.94 = (s16[2,16,208,128]{3,2,1,0:T(8,128)(2,1)}, s16[8,400,128]{2,1,0:T(8,128)(2,1)}, bf16[96,64,128]{2,1,0:T(8,128)(2,1)}, bf16[48,64,128]{2,1,0:T(8,128)(2,1)}) custom-call(s32[1,1,576]{2,1,0:T(1,128)} %rows_ref.3, s32[1,1,576]{2,1,0:T(1,128)} %cols_ref.3, s32[1,1]{1,0:T(1,128)S(6)} %copy.10.count_ref, bf16[96,128,128]{2,1,0:T(8,128)(2,1)} %bitcast.10, ...), custom_call_target="tpu_custom_call" | custom-call | flops 19327352832 | bytes 18874368 | tf_op jit(solution)/shard_map/pallas_call | solution.py:541
  69.0 47.6 %shard_map.95 = (f32[64,768]{1,0:T(8,128)}, f32[64,768]{1,0:T(8,128)}, bf16[16,6,64,128]{3,2,1,0:T(8,128)(2,1)}, bf16[8,6,64,128]{3,2,1,0:T(8,128)(2,1)}, bf16[8,6,64,128]{3,2,1,0:T(8,128)(2,1)}) custom-call(f32[64,768]{1,0:T(8,128)} %get-tuple-element.23.ortho_ref, s16[2,16,208,128]{3,2,1,0:T(8,128)(2,1)} %get-tuple-element.26.xr_ref, ...), custom_call_target="tpu_custom_call" | custom-call | tf_op jit(solution)/shard_map/pallas_call | solution.py:768
  116.7 5.0 %all-to-all-start = ((bf16[16,6,64,128]{3,2,1,0:T(8,128)(2,1)}), bf16[16,6,64,128]{3,2,1,0:T(8,128)(2,1)S(1)}, u32[]{:S(2)}, u32[]{:S(2)}) async-start(bf16[16,6,64,128]{3,2,1,0:T(8,128)(2,1)} %bitcast.4), calls=%async_computation | async-start | bytes 3145728 | tf_op jit(solution)/shard_map/all_to_all | solution.py:789
  121.7 17.1 %shard_map.96 = (s16[2,16,208,128]{3,2,1,0:T(8,128)(2,1)}, s16[8,400,128]{2,1,0:T(8,128)(2,1)}) custom-call(s32[1,1,576]{2,1,0:T(1,128)} %rows_ref.3, s32[1,1,576]{2,1,0:T(1,128)} %cols_ref.3, s32[1,1]{1,0:T(1,128)S(6)} %copy.10.count_ref, bf16[96,64,128]{2,1,0:T(8,128)(2,1)} %bitcast.11, bf16[48,64,128]{2,1,0:T(8,128)(2,1)} %bitcast.13, ...), custom_call_target="tpu_custom_call" | custom-call | flops 9663676416 | bytes 18874368 | tf_op jit(solution)/shard_map/pallas_call | solution.py:541
  138.8 9.7 %all-to-all-done.pr_ref = bf16[16,6,64,128]{3,2,1,0:T(8,128)(2,1)S(1)} async-done(((bf16[16,6,64,128]{3,2,1,0:T(8,128)(2,1)}), bf16[16,6,64,128]{3,2,1,0:T(8,128)(2,1)S(1)}, u32[]{:S(2)}, u32[]{:S(2)}) %all-to-all-start) | async-done | bytes 1572896 | tf_op jit(solution)/shard_map/all_to_all | solution.py:789
  148.5 0.0 copy-start
  148.5 1.1 copy-done
  149.6 41.0 %shard_map.97 = (f32[64,768]{1,0:T(8,128)}, f32[192,384]{1,0:T(8,128)}, f32[192,128]{1,0:T(8,128)}) custom-call(f32[64,768]{1,0:T(8,128)} %get-tuple-element.23.ortho_ref, f32[64,768]{1,0:T(8,128)} %get-tuple-element.29.residual_ref.residual_in, f32[64,768]{1,0:T(8,128)} %p_ref.3, f32[64,768]{1,0:T(8,128)} %get-tuple-element.30.image_x_ref, ...), custom_call_target="tpu_custom_call" | custom-call | tf_op jit(solution)/shard_map/pallas_call | solution.py:802
  190.6 2.1 %shard_map.98 = (f32[64,768]{1,0:T(8,128)}, f32[64,768]{1,0:T(8,128)}, f32[192,192]{1,0:T(8,128)}, f32[192,192]{1,0:T(8,128)}) custom-call(f32[64,768]{1,0:T(8,128)} %get-tuple-element.29.residual_ref.residual_in, f32[64,768]{1,0:T(8,128)} %get-tuple-element.39.image_in, f32[192,384]{1,0:T(8,128)} %get-tuple-element.40.early_ref, ...), custom_call_target="tpu_custom_call" | custom-call | tf_op jit(solution)/shard_map/pallas_call | solution.py:816
Async XLA Ops:
  116.7 31.8 %all-to-all-start = ((bf16[16,6,64,128]{3,2,1,0:T(8,128)(2,1)}), bf16[16,6,64,128]{3,2,1,0:T(8,128)(2,1)S(1)}, u32[]{:S(2)}, u32[]{:S(2)}) async-start(bf16[16,6,64,128]{3,2,1,0:T(8,128)(2,1)} %bitcast.4), calls=%async_computation | async-start | bytes 3145728 | tf_op jit(solution)/shard_map/all_to_all | solution.py:789
  148.5 1.1 copy-start

commit v3 on v2

--- a/solution.py
+++ b/solution.py
@@ -105,6 +105,10 @@
 
 def pack(parts, ref):
     width = parts[0].shape[0]
+    if ref.dtype == BF16:
+        for i, part in enumerate(parts):
+            ref[i * width : (i + 1) * width, :] = part.astype(BF16)
+        return
     most = jnp.abs(parts[0])
     for part in parts[1:]:
         most = jnp.maximum(most, jnp.abs(part))
@@ -121,6 +125,8 @@
 
 
 def unpack(ref, count, width):
+    if ref.dtype == BF16:
+        return [ref[i * width : (i + 1) * width, :].astype(F32) for i in range(count)]
     line = ref[count * width :, :].astype(jnp.int32).astype(F32)[:1]
     down = lax.broadcasted_iota(jnp.int32, (width, TILE), 0)
     across = lax.broadcasted_iota(jnp.int32, (width, TILE), 1)
@@ -309,11 +315,14 @@
         self.move.wait_send()
 
 
-def enter(rows, cols):
+def greet(rows, cols):
     barrier = pltpu.get_barrier_semaphore()
     rows.greet(barrier)
     cols.greet(barrier)
-    pl.semaphore_wait(barrier, rows.size + cols.size - 2)
+
+
+def meet(rows, cols):
+    pl.semaphore_wait(pltpu.get_barrier_semaphore(), rows.size + cols.size - 2)
 
 
 def sum_slots(ref, count):
@@ -361,16 +370,24 @@
 
 def first_kernel(
     n_row, n_col, node_count, x_ref, p_ref, ortho_ref, vrow_ref, vcol_ref,
-    low, first, second, ar_row, ar_col, p_row, p_plane, x_row, x_plane, own,
+    low, x, p, first, second, ar_row, ar_col, p_row, p_plane, x_row, x_plane, own, loads,
 ):
     rows, cols = Line("row", n_row), Line("col", n_col)
     plane = Plane(cols)
     k_width, mine = x_ref.shape
     blocks = mine // TILE
-    enter(rows, cols)
+    fetched = [
+        pltpu.make_async_copy(ref, to, loads.at[i]) for i, (ref, to) in enumerate(((x_ref, x), (p_ref, p)))
+    ]
+    for c in fetched:
+        c.start()
+    greet(rows, cols)
+    fetched[0].wait()
+    part = dot_nt(x[...], x[...]) / node_count
+    fetched[1].wait()
     for b in range(blocks):
-        low[b, k_width:, :] = p_ref[:, b * TILE : (b + 1) * TILE].astype(BF16)
-    part = dot_nt(x_ref[...], x_ref[...]) / node_count
+        low[b, k_width:, :] = p[:, b * TILE : (b + 1) * TILE].astype(BF16)
+    meet(rows, cols)
 
     def gathers(band, row_sems, plane_sems):
         across = PlaneGather(
@@ -393,7 +410,7 @@
 
     gram = all_reduce(rows, cols, part, first, second, ar_row, ar_col, give_p)
     p_across.forward()
-    ortho = dot_nn(factor(gram), x_ref[...])
+    ortho = dot_nn(factor(gram), x[...])
     ortho_ref[...] = ortho
     for b in range(blocks):
         low[b, :k_width, :] = ortho[:, b * TILE : (b + 1) * TILE].astype(BF16)
@@ -494,32 +511,29 @@
 
     lax.fori_loop(0, groups, group, 0)
 
-    row_box, col_box = boxes[:2]
-    n_row, n_col = col_box.shape[0], row_box.shape[1]
+    n_row, n_col = boxes[1].shape[0], boxes[0].shape[1]
     blocks = row_blocks // n_col
-
-    def pack_row(c, carry):
-        for half in (0, 1):
-            at = c if half == 0 else lax.rem(c, SIDE) * SIDE + c // SIDE
-            parts = [row_acc[c * blocks + half * HALF + i, :k_width, :] for i in range(HALF)]
-            pack(parts, row_box.at[half, at])
-        return carry
-
-    def pack_col(r, carry):
-        pack([col_acc[r * blocks + i, :k_width, :] for i in range(blocks)], col_box.at[r])
-        return carry
-
     results = [
         pltpu.make_async_copy(box, out, out_sems.at[i]) for i, (box, out) in enumerate(zip(boxes, outs))
     ]
-    lax.fori_loop(0, n_col, pack_row, 0)
-    results[0].start()
-    lax.fori_loop(0, n_row, pack_col, 0)
-    results[1].start()
-    for i in range(2, n_out):
-        acc, n = ((row_acc, row_blocks), (col_acc, col_blocks))[i - 2]
-        boxes[i][...] = acc[:n, k_width:, :].astype(boxes[i].dtype)
+    for i in range(n_out - 2, -1, -2):
+        band = pl.ds(i // 2 * k_width, k_width)
+
+        def pack_row(c, carry):
+            for half in (0, 1):
+                at = c if half == 0 else lax.rem(c, SIDE) * SIDE + c // SIDE
+                parts = [row_acc[c * blocks + half * HALF + n, band, :] for n in range(HALF)]
+                pack(parts, boxes[i].at[half, at])
+            return carry
+
+        def pack_col(r, carry):
+            pack([col_acc[r * blocks + n, band, :] for n in range(blocks)], boxes[i + 1].at[r])
+            return carry
+
+        lax.fori_loop(0, n_col, pack_row, 0)
         results[i].start()
+        lax.fori_loop(0, n_row, pack_col, 0)
+        results[i + 1].start()
     for c in results:
         c.wait()
 
@@ -537,7 +551,10 @@
         shape((n_row, blocks * k_width + SPARE, TILE), jnp.int16),
     ]
     if width > k_width:
-        out_shape += [shape((n, width - k_width, TILE), BF16) for n in (row_blocks, col_blocks)]
+        out_shape += [
+            shape((2, n_col, HALF * k_width, TILE), BF16),
+            shape((n_row, blocks * k_width, TILE), BF16),
+        ]
     return pl.pallas_call(
         functools.partial(apply_kernel, k_width),
         in_specs=[smem] * 3 + [anywhere] * 3,
@@ -567,30 +584,40 @@
 
 
 def middle_kernel(
-    n_row, n_col, node_count, ortho_ref, xr_ref, xc_ref, pc_ref,
-    residual_ref, image_x_ref, vrow_ref, vcol_ref, p_box_ref,
-    first_in, second_in, second_out, inbox, low, first, second,
-    s1, s2, s_row, ar_row, ar_col, g_row, g_plane, p_row, own,
+    n_row, n_col, node_count, ortho_ref, xr_ref, xc_ref, pr_ref, pc_ref,
+    residual_ref, image_x_ref, image_p_ref, vrow_ref, vcol_ref,
+    first_in, second_in, second_out, inbox, p_first_in, p_second_in, p_second_out, p_inbox,
+    ortho, low, first, second,
+    s1, s2, s_row, p1, p2, p_row, ar_row, ar_col, g_row, g_plane, own, loads,
 ):
     rows, cols = Line("row", n_row), Line("col", n_col)
     plane = Plane(cols)
     k_width, mine = ortho_ref.shape
     blocks = mine // TILE
-    enter(rows, cols)
+    fetched = pltpu.make_async_copy(ortho_ref, ortho, loads.at[0])
+    fetched.start()
+    greet(rows, cols)
+    meet(rows, cols)
     across = PlaneSum(plane, xr_ref, first_in, second_in, second_out, s1, s2, own)
     along = RowSum(rows, xc_ref, inbox, s_row, own.at[2])
+    p_across = PlaneSum(plane, pr_ref, p_first_in, p_second_in, p_second_out, p1, p2, loads.at[pl.ds(1, 2)])
+    p_along = RowSum(rows, pc_ref, p_inbox, p_row, loads.at[3])
     across.start()
     along.start()
     across.pass_on(k_width)
+    p_across.start()
     from_rows = along.finish(blocks, k_width)
     images = add_lists([across.finish(k_width), from_rows])
-    image = jnp.concatenate(images, axis=1)
-    image_x_ref[...] = image
-    ortho = ortho_ref[...]
-    part = dot_nt(ortho, image) / node_count
-    p_along = Exchange(rows, lambda p: pc_ref.at[p], lambda s: p_box_ref.at[s], p_row)
-    rayleigh = all_reduce(rows, cols, part, first, second, ar_row, ar_col, p_along.start)
-    residual = image_x_ref[...] - dot_tn(rayleigh, ortho)
+    image_x_ref[...] = jnp.concatenate(images, axis=1)
+    fetched.wait()
+    part = dot_nt(ortho[...], image_x_ref[...]) / node_count
+
+    def meanwhile():
+        p_across.pass_on(k_width)
+        p_along.start()
+
+    rayleigh = all_reduce(rows, cols, part, first, second, ar_row, ar_col, meanwhile)
+    residual = image_x_ref[...] - dot_tn(rayleigh, ortho[...])
     residual_ref[...] = residual
     for b in range(blocks):
         low[b] = residual[:, b * TILE : (b + 1) * TILE].astype(BF16)
@@ -606,17 +633,17 @@
     here = [
         pltpu.make_async_copy(low, vrow_ref.at[cols.me], own.at[3]),
         pltpu.make_async_copy(low, vcol_ref.at[rows.me], own.at[4]),
-        pltpu.make_async_copy(pc_ref.at[rows.me], p_box_ref.at[rows.me], own.at[5]),
     ]
     for c in here:
         c.start()
     g_across.forward()
+    p_images = add_lists([p_across.finish(k_width), p_along.finish(blocks, k_width)])
+    image_p_ref[...] = jnp.concatenate(p_images, axis=1)
     g_across.wait_recv()
     g_along.wait_recv()
-    p_along.wait_recv()
     for c in here:
         c.wait()
-    for c in (across, along, g_across, g_along, p_along):
+    for c in (across, along, p_across, p_along, g_across, g_along):
         c.wait_send()
 
 
@@ -654,48 +681,46 @@
 
 
 def last_kernel(
-    n_row, n_col, node_count, ortho_ref, residual_ref, p_ref, image_x_ref, pr_ref, pc_ref,
+    n_row, n_col, node_count, ortho_ref, residual_ref, p_ref, image_x_ref, image_p_ref,
     rr_ref, rc_ref, image_r_ref, early_ref, late_ref,
-    first_in, second_in, second_out, inbox,
+    first_in, second_in, second_out, inbox, basis, image_x, image_p,
     e_whole, e_first, e_second, e_done, l_whole, l_first, l_second, l_done,
-    s1, s2, s_row, e1, e2, e3, l1, l2, l3, own,
+    s1, s2, s_row, e1, e2, e3, l1, l2, l3, own, loads,
 ):
     rows, cols = Line("row", n_row), Line("col", n_col)
     plane = Plane(cols)
     k_width, mine = ortho_ref.shape
     blocks = mine // TILE
-    enter(rows, cols)
+    sources = [(r, basis.at[pl.ds(i * k_width, k_width)]) for i, r in enumerate((ortho_ref, residual_ref, p_ref))]
+    sources += [(image_x_ref, image_x), (image_p_ref, image_p)]
+    fetched = [pltpu.make_async_copy(r, to, loads.at[i]) for i, (r, to) in enumerate(sources)]
+    for c in fetched:
+        c.start()
+    greet(rows, cols)
+    meet(rows, cols)
     across = PlaneSum(plane, rr_ref, first_in, second_in, second_out, s1, s2, own)
     along = RowSum(rows, rc_ref, inbox, s_row, own.at[2])
     across.start()
     along.start()
-    basis = jnp.concatenate([ortho_ref[...], residual_ref[...], p_ref[...]], axis=0)
-    image_p = []
-    for b in range(blocks):
-        total = pr_ref[0, b].astype(F32)
-        for j in range(1, n_col):
-            total = total + pr_ref[j, b].astype(F32)
-        for j in range(n_row):
-            total = total + pc_ref[j, b].astype(F32)
-        image_p.append(total)
-    others = jnp.concatenate([image_x_ref[...], jnp.concatenate(image_p, axis=1)], axis=0)
-    e_whole[:, : 2 * k_width] = dot_nt(basis, others) / node_count
-    gram_b = dot_nt(basis, basis) / node_count
-    pad = jnp.zeros((3 * k_width, k_width), F32)
-    e_whole[:, 2 * k_width :] = jnp.concatenate([gram_b, pad], axis=1)
+    for c in fetched:
+        c.wait()
+    e_whole[:, : 3 * k_width] = dot_nt(basis[...], basis[...]) / node_count
+    e_whole[:, 3 * k_width :] = dot_nt(basis[...], image_x[...]) / node_count
     early = Spread(rows, cols, e_whole, e_first, e_second, e_done, (e1, e2, e3))
     late = Spread(rows, cols, l_whole, l_first, l_second, l_done, (l1, l2, l3))
     early.start()
+    from_p = dot_nt(basis[...], image_p[...]) / node_count
     across.pass_on(k_width)
     early.turn()
     from_rows = along.finish(blocks, k_width)
     images = add_lists([across.finish(k_width), from_rows])
     image_r = jnp.concatenate(images, axis=1)
     image_r_ref[...] = image_r
-    l_whole[...] = jnp.concatenate([dot_nt(basis, image_r) / node_count, pad], axis=1)
+    from_r = dot_nt(basis[...], image_r) / node_count
+    l_whole[...] = jnp.concatenate([from_r, from_p], axis=1)
     late.start()
+    late.turn()
     early.back()
-    late.turn()
     late.back()
     early.finish()
     early_ref[...] = e_done[...]
@@ -709,9 +734,8 @@
     residual_ref[...] = residual_in[...]
     image_ref[...] = image_in[...]
     k_width = residual_in.shape[0]
-    x_cols, p_cols = early_ref[:, :k_width], early_ref[:, k_width : 2 * k_width]
-    a_ref[...] = jnp.concatenate([x_cols, late_ref[:, :k_width], p_cols], axis=1)
-    b_ref[...] = early_ref[:, 2 * k_width : 5 * k_width]
+    a_ref[...] = jnp.concatenate([early_ref[:, 3 * k_width :], late_ref[...]], axis=1)
+    b_ref[...] = early_ref[:, : 3 * k_width]
 
 
 def per_device(block_x, block_p, tile_rows, tile_cols, tile_count, tile_vals):
@@ -746,7 +770,7 @@
 
     ortho, vrow, vcol = pl.pallas_call(
         functools.partial(first_kernel, n_row, n_col, node_count),
-        in_specs=[vmem] * 2,
+        in_specs=[anywhere] * 2,
         out_specs=[vmem, anywhere, anywhere],
         out_shape=[
             local,
@@ -755,40 +779,43 @@
         ],
         scratch_shapes=[
             pltpu.VMEM((blocks, 2 * k_width, TILE), BF16),
+            pltpu.VMEM((k_width, mine), F32),
+            pltpu.VMEM((k_width, mine), F32),
             *small,
             row_sems, col_sems, row_sems, plane_sems, row_sems, plane_sems,
+            pltpu.SemaphoreType.DMA((2,)),
             pltpu.SemaphoreType.DMA((2,)),
         ],
         compiler_params=params(0),
     )(block_x, block_p)
 
     xr, xc, pr, pc = apply_graph(tile_rows, tile_cols, tile_count, vrow, vcol, vals, k_width)
-    pc = pc.reshape(n_row, blocks, k_width, TILE)
-
-    residual, image_x, vrow, vcol, pc = pl.pallas_call(
+
+    residual, image_x, image_p, vrow, vcol = pl.pallas_call(
         functools.partial(middle_kernel, n_row, n_col, node_count),
-        in_specs=[vmem] + [anywhere] * 3,
-        out_specs=[vmem, vmem] + [anywhere] * 3,
+        in_specs=[anywhere] * 5,
+        out_specs=[vmem] * 3 + [anywhere] * 2,
         out_shape=[
-            local, local,
+            local, local, local,
             shape((n_col, blocks, k_width, TILE), BF16),
-            shape((n_row, blocks, k_width, TILE), BF16),
             shape((n_row, blocks, k_width, TILE), BF16),
         ],
         scratch_shapes=[
             *sum_boxes,
+            pltpu.VMEM((2, SIDE, SIDE, HALF * k_width, TILE), BF16),
+            pltpu.VMEM((2, SIDE, HALF * k_width, TILE), BF16),
+            pltpu.VMEM((2, SIDE, HALF * k_width, TILE), BF16),
+            pltpu.VMEM((n_row, blocks * k_width, TILE), BF16),
+            pltpu.VMEM((k_width, mine), F32),
             pltpu.VMEM((blocks, k_width, TILE), BF16),
             *small,
-            plane_sems, ring_sems, row_sems, row_sems, col_sems, row_sems, plane_sems, row_sems,
-            pltpu.SemaphoreType.DMA((6,)),
+            plane_sems, ring_sems, row_sems, plane_sems, ring_sems, row_sems,
+            row_sems, col_sems, row_sems, plane_sems,
+            pltpu.SemaphoreType.DMA((5,)),
+            pltpu.SemaphoreType.DMA((4,)),
         ],
         compiler_params=params(1),
-    )(ortho, xr, xc, pc)
-
-    pr, vcol = lax.optimization_barrier((pr, vcol))
-    pr = lax.all_to_all(
-        pr.reshape(n_col, blocks, k_width, TILE), "col", split_axis=0, concat_axis=0, tiled=True
-    )
+    )(ortho, xr, xc, pr, pc)
 
     rr, rc = apply_graph(tile_rows, tile_cols, tile_count, vrow, vcol, vals, k_width)
 
@@ -801,17 +828,22 @@
     ]
     image_r, early, late = pl.pallas_call(
         functools.partial(last_kernel, n_row, n_col, node_count),
-        in_specs=[vmem] * 6 + [anywhere] * 2,
+        in_specs=[anywhere] * 7,
         out_specs=[vmem] * 3,
-        out_shape=[local, shape((full, 6 * k_width), F32), shape((full, 2 * k_width), F32)],
+        out_shape=[local, shape((full, 4 * k_width), F32), shape((full, 2 * k_width), F32)],
         scratch_shapes=[
-            *sum_boxes, *spread(6 * k_width), *spread(2 * k_width),
+            *sum_boxes,
+            pltpu.VMEM((full, mine), F32),
+            pltpu.VMEM((k_width, mine), F32),
+            pltpu.VMEM((k_width, mine), F32),
+            *spread(4 * k_width), *spread(2 * k_width),
             plane_sems, ring_sems, row_sems,
             row_sems, col_sems, row_sems, row_sems, col_sems, row_sems,
             pltpu.SemaphoreType.DMA((3,)),
+            pltpu.SemaphoreType.DMA((5,)),
         ],
         compiler_params=params(2),
-    )(ortho, residual, block_p, image_x, pr, pc, rr, rc)
+    )(ortho, residual, block_p, image_x, image_p, rr, rc)
     return tuple(
         pl.pallas_call(
             hand_kernel,

time: 193 us -> 173 us (0.90)
  waiting for transfers between devices: 9.67 us -> 0 us
  Pallas kernels: 176 us -> 171 us
  starting transfers between devices: 4.99 us -> 0 us
    all_to_all x1 -> x0, waiting for transfers between devices: 9.67 us -> none  [per_device(): lax.all_to_all(pr.reshape(n_col, blocks, k_width, TILE), 'col', split_axi...]
    pallas_call x1, Pallas kernels: 41 us -> 35.7 us  [per_device(): pl.pallas_call(functools.partial(last_kernel, n_row, n_col, node_count),...]
    all_to_all x1 -> x0, starting transfers between devices: 4.99 us -> none  [per_device(): lax.all_to_all(pr.reshape(n_col, blocks, k_width, TILE), 'col', split_axi...]
    pallas_call x1, Pallas kernels: 47.6 us -> 50.2 us  [per_device(): pl.pallas_call(functools.partial(middle_kernel, n_row, n_col, node_count)...]
  transfers between devices with their start and end apart: 1 -> 0, of which waited for: 1 -> 0; matrix products, arithmetic and copies ran while one was open for 0% -> 0% of each run, Pallas kernels for 9% -> 0%
where the time goes in v3:
time: 173 us; the launch traced here: 172 us
  Pallas kernels  171 us (99%)
    pallas_call x1, Pallas kernels, per_device(): pl.pallas_call(functools.partial(middle_kernel, n_row, n_col, node_count)...  50.2 us
    pallas_call x1, Pallas kernels, per_device(): pl.pallas_call(functools.partial(first_kernel, n_row, n_col, node_count),...  43.1 us
    pallas_call x2, Pallas kernels, apply_graph(): pl.pallas_call(functools.partial(apply_kernel, k_width), in_specs=[smem]...  39.9 us
    pallas_call x1, Pallas kernels, per_device(): pl.pallas_call(functools.partial(last_kernel, n_row, n_col, node_count),...  35.7 us

profile of v3, /device:TPU:1, one launch (start us, length us, event | category | flops | bytes accessed | tf_op | source)
XLA Modules:
  0.0 172.4 jit_solution(8385111688649724187)
XLA Ops:
  1.3 43.1 %shard_map.93 = (f32[64,768]{1,0:T(8,128)}, bf16[16,6,128,128]{3,2,1,0:T(8,128)(2,1)}, bf16[8,6,128,128]{3,2,1,0:T(8,128)(2,1)}) custom-call(f32[64,768]{1,0:T(8,128)} %x_ref.1, f32[64,768]{1,0:T(8,128)} %p_ref.3), custom_call_target="tpu_custom_call" | custom-call | tf_op jit(solution)/shard_map/pallas_call | solution.py:771
  44.4 22.8 %shard_map.94 = (s16[2,16,208,128]{3,2,1,0:T(8,128)(2,1)}, s16[8,400,128]{2,1,0:T(8,128)(2,1)}, bf16[2,16,192,128]{3,2,1,0:T(8,128)(2,1)}, bf16[8,384,128]{2,1,0:T(8,128)(2,1)}) custom-call(s32[1,1,576]{2,1,0:T(1,128)} %rows_ref.3, s32[1,1,576]{2,1,0:T(1,128)} %cols_ref.3, s32[1,1]{1,0:T(1,128)S(6)} %copy.10.count_ref, bf16[96,128,128]{2,1,0:T(8,128)(2,1)} %bitcast.7, ...), custom_call_target="tpu_custom_call" | custom-call | flops 19327352832 | bytes 18874368 | tf_op jit(solution)/shard_map/pallas_call | solution.py:558
  67.2 50.2 %shard_map.95 = (f32[64,768]{1,0:T(8,128)}, f32[64,768]{1,0:T(8,128)}, f32[64,768]{1,0:T(8,128)}, bf16[16,6,64,128]{3,2,1,0:T(8,128)(2,1)}, bf16[8,6,64,128]{3,2,1,0:T(8,128)(2,1)}) custom-call(f32[64,768]{1,0:T(8,128)} %get-tuple-element.21.ortho_ref, s16[2,16,208,128]{3,2,1,0:T(8,128)(2,1)} %get-tuple-element.24.xr_ref, ...), custom_call_target="tpu_custom_call" | custom-call | tf_op jit(solution)/shard_map/pallas_call | solution.py:794
  117.4 17.1 %shard_map.96 = (s16[2,16,208,128]{3,2,1,0:T(8,128)(2,1)}, s16[8,400,128]{2,1,0:T(8,128)(2,1)}) custom-call(s32[1,1,576]{2,1,0:T(1,128)} %rows_ref.3, s32[1,1,576]{2,1,0:T(1,128)} %cols_ref.3, s32[1,1]{1,0:T(1,128)S(6)} %copy.10.count_ref, bf16[96,64,128]{2,1,0:T(8,128)(2,1)} %bitcast.8, bf16[48,64,128]{2,1,0:T(8,128)(2,1)} %bitcast.10, ...), custom_call_target="tpu_custom_call" | custom-call | flops 9663676416 | bytes 18874368 | tf_op jit(solution)/shard_map/pallas_call | solution.py:558
  134.5 35.7 %shard_map.97 = (f32[64,768]{1,0:T(8,128)}, f32[192,256]{1,0:T(8,128)}, f32[192,128]{1,0:T(8,128)}) custom-call(f32[64,768]{1,0:T(8,128)} %get-tuple-element.21.ortho_ref, f32[64,768]{1,0:T(8,128)} %get-tuple-element.28.residual_ref.residual_in, f32[64,768]{1,0:T(8,128)} %p_ref.3, f32[64,768]{1,0:T(8,128)} %get-tuple-element.29.image_x_ref, ...), custom_call_target="tpu_custom_call" | custom-call | tf_op jit(solution)/shard_map/pallas_call | solution.py:829
  170.3 2.1 %shard_map.98 = (f32[64,768]{1,0:T(8,128)}, f32[64,768]{1,0:T(8,128)}, f32[192,192]{1,0:T(8,128)}, f32[192,192]{1,0:T(8,128)}) custom-call(f32[64,768]{1,0:T(8,128)} %get-tuple-element.28.residual_ref.residual_in, f32[64,768]{1,0:T(8,128)} %get-tuple-element.35.image_in, f32[192,256]{1,0:T(8,128)} %get-tuple-element.36.early_ref, ...), custom_call_target="tpu_custom_call" | custom-call | tf_op jit(solution)/shard_map/pallas_call | solution.py:848

commit v4 on v3

--- a/solution.py
+++ b/solution.py
@@ -12,7 +12,6 @@
 TILE = 128
 HIGHEST = lax.Precision.HIGHEST
 MESH = pl.DeviceIdType.MESH
-VMEM_LIMIT = 56 * 2**20
 GROUP = 48
 SIDE = 4
 HALF = 3
@@ -332,11 +331,16 @@
     return total
 
 
-def all_reduce(rows, cols, part, first, second, row_sems, col_sems, between=None):
+def all_reduce(
+    rows, cols, part, first, second, row_sems, col_sems, between=None, before=None
+):
     half = part.shape[0] // 2
     first[rows.me] = jnp.concatenate([part[:half], part[half:]], axis=1)
     one = Exchange(rows, lambda p: first.at[rows.me], lambda s: first.at[s], row_sems)
-    one.start().wait_recv()
+    one.start()
+    if before is not None:
+        before()
+    one.wait_recv()
     second[cols.me] = sum_slots(first, rows.size)
     two = Exchange(cols, lambda p: second.at[cols.me], lambda s: second.at[s], col_sems)
     two.start()
@@ -404,12 +408,13 @@
     p_across, p_along = gathers(pl.ds(k_width, k_width), p_row, p_plane)
     x_across, x_along = gathers(pl.ds(0, k_width), x_row, x_plane)
 
-    def give_p():
-        p_across.start()
+    def pass_p():
+        p_across.forward()
         p_along.start()
 
-    gram = all_reduce(rows, cols, part, first, second, ar_row, ar_col, give_p)
-    p_across.forward()
+    gram = all_reduce(
+        rows, cols, part, first, second, ar_row, ar_col, pass_p, p_across.start
+    )
     ortho = dot_nn(factor(gram), x[...])
     ortho_ref[...] = ortho
     for b in range(blocks):
@@ -439,11 +444,11 @@
 
 
 def apply_kernel(
-    k_width, rows_ref, cols_ref, count_ref, vrow_ref, vcol_ref, tile_ref, *rest
+    k_width, rows_in, cols_in, count_ref, vrow_ref, vcol_ref, tile_ref, *rest
 ):
-    n_out = (len(rest) - 8) // 2
+    n_out = (len(rest) - 10) // 2
     outs, boxes = rest[:n_out], rest[n_out : 2 * n_out]
-    vrow, vcol, tiles, row_acc, col_acc, tile_sems, in_sems, out_sems = rest[2 * n_out :]
+    rows_ref, cols_ref, vrow, vcol, tiles, row_acc, col_acc, tile_sems, in_sems, out_sems = rest[2 * n_out :]
     row_blocks, width, _ = vrow.shape
     col_blocks = vcol.shape[0]
     count = count_ref[0, 0]
@@ -460,10 +465,12 @@
     inputs = [
         pltpu.make_async_copy(vcol_ref, vcol, in_sems.at[0]),
         pltpu.make_async_copy(vrow_ref, vrow, in_sems.at[1]),
-    ]
-    tile_copy(0).start()
+        pltpu.make_async_copy(rows_in, rows_ref, in_sems.at[2]),
+        pltpu.make_async_copy(cols_in, cols_ref, in_sems.at[3]),
+    ]
     for c in inputs:
         c.start()
+    tile_copy(0).start()
     lax.fori_loop(1, groups, start_copy, 0)
     row_acc[...] = jnp.zeros_like(row_acc)
     col_acc[...] = jnp.zeros_like(col_acc)
@@ -544,6 +551,7 @@
     slots = vals.shape[0]
     row_blocks, col_blocks = n_col * blocks, n_row * blocks
     smem = pl.BlockSpec(memory_space=pltpu.SMEM)
+    in_hbm = pl.BlockSpec(memory_space=pltpu.HBM)
     anywhere = pl.BlockSpec(memory_space=pl.ANY)
     shape = jax.ShapeDtypeStruct
     out_shape = [
@@ -557,21 +565,23 @@
         ]
     return pl.pallas_call(
         functools.partial(apply_kernel, k_width),
-        in_specs=[smem] * 3 + [anywhere] * 3,
+        in_specs=[in_hbm] * 2 + [smem] + [anywhere] * 2 + [in_hbm],
         out_specs=[anywhere] * len(out_shape),
         out_shape=out_shape,
         scratch_shapes=[
             *[pltpu.VMEM(o.shape, o.dtype) for o in out_shape],
+            pltpu.SMEM(tile_rows.shape, jnp.int32),
+            pltpu.SMEM(tile_cols.shape, jnp.int32),
             pltpu.VMEM((row_blocks, width, TILE), BF16),
             pltpu.VMEM((col_blocks, width, TILE), BF16),
             pltpu.VMEM((slots, TILE, TILE), BF16),
             pltpu.VMEM((row_blocks + 1, width, TILE), F32),
             pltpu.VMEM((col_blocks + 1, width, TILE), F32),
             pltpu.SemaphoreType.DMA((slots // GROUP,)),
-            pltpu.SemaphoreType.DMA((2,)),
+            pltpu.SemaphoreType.DMA((4,)),
             pltpu.SemaphoreType.DMA((len(out_shape),)),
         ],
-        compiler_params=pltpu.CompilerParams(vmem_limit_bytes=VMEM_LIMIT),
+        compiler_params=pltpu.CompilerParams(vmem_limit_bytes=(24 + 18 * width // TILE) * 2**20),
         cost_estimate=pl.CostEstimate(
             flops=16 * slots * width * TILE * TILE,
             bytes_accessed=2 * slots * TILE * TILE,
@@ -730,12 +740,21 @@
     along.wait_send()
 
 
-def hand_kernel(residual_in, image_in, early_ref, late_ref, residual_ref, image_ref, a_ref, b_ref):
-    residual_ref[...] = residual_in[...]
-    image_ref[...] = image_in[...]
-    k_width = residual_in.shape[0]
-    a_ref[...] = jnp.concatenate([early_ref[:, 3 * k_width :], late_ref[...]], axis=1)
-    b_ref[...] = early_ref[:, : 3 * k_width]
+def hand_kernel(
+    residual_in, image_in, early_ref, late_ref, residual_ref, image_ref, a_ref, b_ref,
+    early, late, sems,
+):
+    pairs = ((early_ref, early), (late_ref, late), (residual_in, residual_ref), (image_in, image_ref))
+    copies = [pltpu.make_async_copy(r, to, sems.at[i]) for i, (r, to) in enumerate(pairs)]
+    for c in copies:
+        c.start()
+    full = early.shape[0]
+    copies[0].wait()
+    copies[1].wait()
+    a_ref[...] = jnp.concatenate([early[:, full:], late[...]], axis=1)
+    b_ref[...] = early[:, :full]
+    copies[2].wait()
+    copies[3].wait()
 
 
 def per_device(block_x, block_p, tile_rows, tile_cols, tile_count, tile_vals):
@@ -745,15 +764,18 @@
     blocks = mine // TILE
     slots = tile_vals.shape[2]
     vals = tile_vals.reshape(slots, TILE, TILE)
+    keep = lambda v: pltpu.with_memory_space_constraint(v, pltpu.HBM)
+    tile_rows, tile_cols, vals = keep(tile_rows), keep(tile_cols), keep(vals)
     vmem = pl.BlockSpec(memory_space=pltpu.VMEM)
     anywhere = pl.BlockSpec(memory_space=pl.ANY)
+    in_hbm = pl.BlockSpec(memory_space=pltpu.HBM)
     row_sems = pltpu.SemaphoreType.DMA((2, n_row))
     col_sems = pltpu.SemaphoreType.DMA((2, n_col))
     plane_sems = pltpu.SemaphoreType.DMA((2, 2, SIDE, SIDE))
     ring_sems = pltpu.SemaphoreType.DMA((2, 2, SIDE))
     shape = jax.ShapeDtypeStruct
-    params = lambda i: pltpu.CompilerParams(
-        collective_id=i, has_side_effects=True, vmem_limit_bytes=VMEM_LIMIT
+    params = lambda i, mib: pltpu.CompilerParams(
+        collective_id=i, has_side_effects=True, vmem_limit_bytes=mib * 2**20
     )
     local = shape((k_width, mine), F32)
     half_rows, all_rows = HALF * k_width + SPARE, blocks * k_width + SPARE
@@ -770,7 +792,7 @@
 
     ortho, vrow, vcol = pl.pallas_call(
         functools.partial(first_kernel, n_row, n_col, node_count),
-        in_specs=[anywhere] * 2,
+        in_specs=[in_hbm] * 2,
         out_specs=[vmem, anywhere, anywhere],
         out_shape=[
             local,
@@ -786,8 +808,8 @@
             pltpu.SemaphoreType.DMA((2,)),
             pltpu.SemaphoreType.DMA((2,)),
         ],
-        compiler_params=params(0),
-    )(block_x, block_p)
+        compiler_params=params(0, 8),
+    )(keep(block_x), keep(block_p))
 
     xr, xc, pr, pc = apply_graph(tile_rows, tile_cols, tile_count, vrow, vcol, vals, k_width)
 
@@ -814,7 +836,7 @@
             pltpu.SemaphoreType.DMA((5,)),
             pltpu.SemaphoreType.DMA((4,)),
         ],
-        compiler_params=params(1),
+        compiler_params=params(1, 14),
     )(ortho, xr, xc, pr, pc)
 
     rr, rc = apply_graph(tile_rows, tile_cols, tile_count, vrow, vcol, vals, k_width)
@@ -842,14 +864,20 @@
             pltpu.SemaphoreType.DMA((3,)),
             pltpu.SemaphoreType.DMA((5,)),
         ],
-        compiler_params=params(2),
+        compiler_params=params(2, 12),
     )(ortho, residual, block_p, image_x, image_p, rr, rc)
     return tuple(
         pl.pallas_call(
             hand_kernel,
-            in_specs=[vmem] * 4,
-            out_specs=[vmem] * 4,
+            in_specs=[anywhere] * 4,
+            out_specs=[anywhere] * 2 + [vmem] * 2,
             out_shape=[local, local, shape((full, full), F32), shape((full, full), F32)],
+            scratch_shapes=[
+                pltpu.VMEM((full, 4 * k_width), F32),
+                pltpu.VMEM((full, 2 * k_width), F32),
+                pltpu.SemaphoreType.DMA((4,)),
+            ],
+            compiler_params=pltpu.CompilerParams(vmem_limit_bytes=4 * 2**20),
         )(residual, image_r, early, late)
     )
 

time: 173 us -> 165 us (0.954)
  Pallas kernels: 171 us -> 164 us
    pallas_call x3, Pallas kernels: 42 us -> 33.1 us  [the longest x2 31.2 us: apply_graph(): pl.pallas_call(functools.partial(apply_kernel, k_width), in_specs=[in_hbm...]
    pallas_call x1, Pallas kernels: 43.1 us -> 37.4 us  [per_device(): pl.pallas_call(functools.partial(first_kernel, n_row, n_col, node_count),...]
    pallas_call x1, Pallas kernels: 50.2 us -> 54.4 us  [per_device(): pl.pallas_call(functools.partial(middle_kernel, n_row, n_col, node_count)...]
    pallas_call x1, Pallas kernels: 35.7 us -> 38.5 us  [per_device(): pl.pallas_call(functools.partial(last_kernel, n_row, n_col, node_count),...]
where the time goes in v4:
time: 165 us
  Pallas kernels  164 us (99%)
    pallas_call x1, Pallas kernels, per_device(): pl.pallas_call(functools.partial(middle_kernel, n_row, n_col, node_count)...  54.4 us
    pallas_call x1, Pallas kernels, per_device(): pl.pallas_call(functools.partial(last_kernel, n_row, n_col, node_count),...  38.5 us
    pallas_call x1, Pallas kernels, per_device(): pl.pallas_call(functools.partial(first_kernel, n_row, n_col, node_count),...  37.4 us
    pallas_call x2, Pallas kernels, apply_graph(): pl.pallas_call(functools.partial(apply_kernel, k_width), in_specs=[in_hbm...  31.2 us

profile of v4, /device:TPU:1, one launch (start us, length us, event | category | flops | bytes accessed | tf_op | source)
XLA Modules:
  0.0 165.0 jit_solution(415762666816185044)
XLA Ops:
  1.3 37.4 %shard_map.93 = (f32[64,768]{1,0:T(8,128)S(1)}, bf16[16,6,128,128]{3,2,1,0:T(8,128)(2,1)S(1)}, bf16[8,6,128,128]{3,2,1,0:T(8,128)(2,1)S(1)}) custom-call(f32[64,768]{1,0:T(8,128)} %x_ref.1, f32[64,768]{1,0:T(8,128)} %p_ref.3), custom_call_target="tpu_custom_call" | custom-call | tf_op jit(solution)/shard_map/pallas_call | solution.py:793
  38.7 17.8 %shard_map.94 = (s16[2,16,208,128]{3,2,1,0:T(8,128)(2,1)S(1)}, s16[8,400,128]{2,1,0:T(8,128)(2,1)S(1)}, bf16[2,16,192,128]{3,2,1,0:T(8,128)(2,1)S(1)}, bf16[8,384,128]{2,1,0:T(8,128)(2,1)S(1)}) custom-call(s32[1,1,576]{2,1,0:T(1,128)} %rows_in.3, s32[1,1,576]{2,1,0:T(1,128)} %cols_in.3, s32[1,1]{1,0:T(1,128)S(6)} %copy.10.count_ref, ...), custom_call_target="tpu_custom_call" | custom-call | flops 19327352832 | bytes 18874368 | tf_op jit(solution)/shard_map/pallas_call | solution.py:566
  56.5 54.4 %shard_map.95 = (f32[64,768]{1,0:T(8,128)S(1)}, f32[64,768]{1,0:T(8,128)S(1)}, f32[64,768]{1,0:T(8,128)S(1)}, bf16[16,6,64,128]{3,2,1,0:T(8,128)(2,1)S(1)}, bf16[8,6,64,128]{3,2,1,0:T(8,128)(2,1)S(1)}) custom-call(f32[64,768]{1,0:T(8,128)S(1)} %get-tuple-element.21.ortho_ref, s16[2,16,208,128]{3,2,1,0:T(8,128)(2,1)S(1)} %get-tuple-element.24.xr_ref, ...), custom_call_target="tpu_custom_call" | custom-call | tf_op jit(solution)/shard_map/pallas_call | solution.py:816
  110.9 0.0 copy-start
  111.0 13.4 %shard_map.96 = (s16[2,16,208,128]{3,2,1,0:T(8,128)(2,1)S(1)}, s16[8,400,128]{2,1,0:T(8,128)(2,1)S(1)}) custom-call(s32[1,1,576]{2,1,0:T(1,128)} %rows_in.3, s32[1,1,576]{2,1,0:T(1,128)} %cols_in.3, s32[1,1]{1,0:T(1,128)S(6)} %copy.10.count_ref, bf16[96,64,128]{2,1,0:T(8,128)(2,1)S(1)} %bitcast.6, bf16[48,64,128]{2,1,0:T(8,128)(2,1)S(1)} %bitcast.8, ...), custom_call_target="tpu_custom_call" | custom-call | flops 9663676416 | bytes 18874368 | tf_op jit(solution)/shard_map/pallas_call | solution.py:566
  124.4 0.0 copy-done
  124.4 38.5 %shard_map.97 = (f32[64,768]{1,0:T(8,128)S(1)}, f32[192,256]{1,0:T(8,128)S(1)}, f32[192,128]{1,0:T(8,128)S(1)}) custom-call(f32[64,768]{1,0:T(8,128)S(1)} %get-tuple-element.21.ortho_ref, f32[64,768]{1,0:T(8,128)S(1)} %get-tuple-element.28.residual_ref.residual_in, f32[64,768]{1,0:T(8,128)S(1)} %copy-done, f32[64,768]{1,0:T(8,128)S(1)} %get-tuple-element.29.image_x_ref, ...), custom_call_target="tpu_custom_call" | custom-call | tf_op jit(solution)/shard_map/pallas_call | solution.py:851
  163.0 1.9 %shard_map.98 = (f32[64,768]{1,0:T(8,128)}, f32[64,768]{1,0:T(8,128)}, f32[192,192]{1,0:T(8,128)}, f32[192,192]{1,0:T(8,128)}) custom-call(f32[64,768]{1,0:T(8,128)S(1)} %get-tuple-element.28.residual_ref.residual_in, f32[64,768]{1,0:T(8,128)S(1)} %get-tuple-element.35.image_in, f32[192,256]{1,0:T(8,128)S(1)} %get-tuple-element.36.early_ref, ...), custom_call_target="tpu_custom_call" | custom-call | tf_op jit(solution)/shard_map/pallas_call | solution.py:870
Async XLA Ops:
  110.9 13.5 %copy-start = (f32[64,768]{1,0:T(8,128)S(1)}, f32[64,768]{1,0:T(8,128)}, u32[]{:S(2)}) copy-start(f32[64,768]{1,0:T(8,128)} %p_ref.3) | copy-start | bytes 589828

commit v5 on v4

--- a/solution.py
+++ b/solution.py
@@ -13,6 +13,7 @@
 HIGHEST = lax.Precision.HIGHEST
 MESH = pl.DeviceIdType.MESH
 GROUP = 48
+WIDE_GROUP = 96
 SIDE = 4
 HALF = 3
 SPARE = 16
@@ -444,18 +445,19 @@
 
 
 def apply_kernel(
-    k_width, rows_in, cols_in, count_ref, vrow_ref, vcol_ref, tile_ref, *rest
+    k_width, rows_in, cols_in, count_ref, vrow, vcol, tile_ref, *rest
 ):
-    n_out = (len(rest) - 10) // 2
+    n_out = (len(rest) - 8) // 2
     outs, boxes = rest[:n_out], rest[n_out : 2 * n_out]
-    rows_ref, cols_ref, vrow, vcol, tiles, row_acc, col_acc, tile_sems, in_sems, out_sems = rest[2 * n_out :]
+    rows_ref, cols_ref, tiles, row_acc, col_acc, tile_sems, in_sems, out_sems = rest[2 * n_out :]
     row_blocks, width, _ = vrow.shape
     col_blocks = vcol.shape[0]
     count = count_ref[0, 0]
-    groups = (count + GROUP - 1) // GROUP
+    size = tiles.shape[0] // tile_sems.shape[0]
+    groups = (count + size - 1) // size
 
     def tile_copy(g):
-        part = pl.ds(g * GROUP, GROUP)
+        part = pl.ds(g * size, size)
         return pltpu.make_async_copy(tile_ref.at[part], tiles.at[part], tile_sems.at[g])
 
     def start_copy(g, carry):
@@ -463,10 +465,8 @@
         return carry
 
     inputs = [
-        pltpu.make_async_copy(vcol_ref, vcol, in_sems.at[0]),
-        pltpu.make_async_copy(vrow_ref, vrow, in_sems.at[1]),
-        pltpu.make_async_copy(rows_in, rows_ref, in_sems.at[2]),
-        pltpu.make_async_copy(cols_in, cols_ref, in_sems.at[3]),
+        pltpu.make_async_copy(rows_in, rows_ref, in_sems.at[0]),
+        pltpu.make_async_copy(cols_in, cols_ref, in_sems.at[1]),
     ]
     for c in inputs:
         c.start()
@@ -509,11 +509,11 @@
     def group(g, carry):
         tile_copy(g).wait()
         if width < TILE:
-            for u in range(0, GROUP, 2):
-                pair(g * GROUP + u)
+            for u in range(0, size, 2):
+                pair(g * size + u)
         else:
-            for u in range(GROUP):
-                single(g * GROUP + u)
+            for u in range(size):
+                single(g * size + u)
         return carry
 
     lax.fori_loop(0, groups, group, 0)
@@ -551,6 +551,8 @@
     slots = vals.shape[0]
     row_blocks, col_blocks = n_col * blocks, n_row * blocks
     smem = pl.BlockSpec(memory_space=pltpu.SMEM)
+    vmem = pl.BlockSpec(memory_space=pltpu.VMEM)
+    near = lambda v: pltpu.with_memory_space_constraint(v, pltpu.VMEM)
     in_hbm = pl.BlockSpec(memory_space=pltpu.HBM)
     anywhere = pl.BlockSpec(memory_space=pl.ANY)
     shape = jax.ShapeDtypeStruct
@@ -565,20 +567,18 @@
         ]
     return pl.pallas_call(
         functools.partial(apply_kernel, k_width),
-        in_specs=[in_hbm] * 2 + [smem] + [anywhere] * 2 + [in_hbm],
+        in_specs=[in_hbm] * 2 + [smem] + [vmem] * 2 + [in_hbm],
         out_specs=[anywhere] * len(out_shape),
         out_shape=out_shape,
         scratch_shapes=[
             *[pltpu.VMEM(o.shape, o.dtype) for o in out_shape],
             pltpu.SMEM(tile_rows.shape, jnp.int32),
             pltpu.SMEM(tile_cols.shape, jnp.int32),
-            pltpu.VMEM((row_blocks, width, TILE), BF16),
-            pltpu.VMEM((col_blocks, width, TILE), BF16),
             pltpu.VMEM((slots, TILE, TILE), BF16),
             pltpu.VMEM((row_blocks + 1, width, TILE), F32),
             pltpu.VMEM((col_blocks + 1, width, TILE), F32),
-            pltpu.SemaphoreType.DMA((slots // GROUP,)),
-            pltpu.SemaphoreType.DMA((4,)),
+            pltpu.SemaphoreType.DMA((slots // (GROUP if width == TILE else WIDE_GROUP),)),
+            pltpu.SemaphoreType.DMA((2,)),
             pltpu.SemaphoreType.DMA((len(out_shape),)),
         ],
         compiler_params=pltpu.CompilerParams(vmem_limit_bytes=(24 + 18 * width // TILE) * 2**20),
@@ -589,7 +589,9 @@
         ),
     )(
         tile_rows, tile_cols, count,
-        vrow.reshape(row_blocks, width, TILE), vcol.reshape(col_blocks, width, TILE), vals,
+        near(vrow.reshape(row_blocks, width, TILE)),
+        near(vcol.reshape(col_blocks, width, TILE)),
+        vals,
     )
 
 

time: 165 us -> 164 us (level)
    pallas_call x2, Pallas kernels: 31.2 us -> 35 us  [apply_graph(): pl.pallas_call(functools.partial(apply_kernel, k_width), in_specs=[in_hbm...]
    pallas_call x1, Pallas kernels: 54.4 us -> 51.5 us  [per_device(): pl.pallas_call(functools.partial(middle_kernel, n_row, n_col, node_count)...]
where the time goes in v5:
time: 164 us
  Pallas kernels  163 us (99%)
    pallas_call x1, Pallas kernels, per_device(): pl.pallas_call(functools.partial(middle_kernel, n_row, n_col, node_count)...  51.5 us
    pallas_call x1, Pallas kernels, per_device(): pl.pallas_call(functools.partial(first_kernel, n_row, n_col, node_count),...  37.4 us
    pallas_call x1, Pallas kernels, per_device(): pl.pallas_call(functools.partial(last_kernel, n_row, n_col, node_count),...  36.9 us
    pallas_call x2, Pallas kernels, apply_graph(): pl.pallas_call(functools.partial(apply_kernel, k_width), in_specs=[in_hbm...  35 us

profile of v5, /device:TPU:1, one launch (start us, length us, event | category | flops | bytes accessed | tf_op | source)
XLA Modules:
  0.0 164.3 jit_solution(12932568406119684909)
XLA Ops:
  1.3 37.4 %shard_map.93 = (f32[64,768]{1,0:T(8,128)S(1)}, bf16[16,6,128,128]{3,2,1,0:T(8,128)(2,1)S(1)}, bf16[8,6,128,128]{3,2,1,0:T(8,128)(2,1)S(1)}) custom-call(f32[64,768]{1,0:T(8,128)} %x_ref.1, f32[64,768]{1,0:T(8,128)} %p_ref.3), custom_call_target="tpu_custom_call" | custom-call | tf_op jit(solution)/shard_map/pallas_call | solution.py:795
  38.7 20.3 %shard_map.94 = (s16[2,16,208,128]{3,2,1,0:T(8,128)(2,1)S(1)}, s16[8,400,128]{2,1,0:T(8,128)(2,1)S(1)}, bf16[2,16,192,128]{3,2,1,0:T(8,128)(2,1)S(1)}, bf16[8,384,128]{2,1,0:T(8,128)(2,1)S(1)}) custom-call(s32[1,1,576]{2,1,0:T(1,128)} %rows_in.3, s32[1,1,576]{2,1,0:T(1,128)} %cols_in.3, s32[1,1]{1,0:T(1,128)S(6)} %copy.10.count_ref, ...), custom_call_target="tpu_custom_call" | custom-call | flops 19327352832 | bytes 18874368 | tf_op jit(solution)/shard_map/pallas_call | solution.py:568
  59.1 51.5 %shard_map.95 = (f32[64,768]{1,0:T(8,128)S(1)}, f32[64,768]{1,0:T(8,128)S(1)}, f32[64,768]{1,0:T(8,128)S(1)}, bf16[16,6,64,128]{3,2,1,0:T(8,128)(2,1)S(1)}, bf16[8,6,64,128]{3,2,1,0:T(8,128)(2,1)S(1)}) custom-call(f32[64,768]{1,0:T(8,128)S(1)} %get-tuple-element.21.ortho_ref, s16[2,16,208,128]{3,2,1,0:T(8,128)(2,1)S(1)} %get-tuple-element.24.xr_ref, ...), custom_call_target="tpu_custom_call" | custom-call | tf_op jit(solution)/shard_map/pallas_call | solution.py:818
  110.6 0.0 copy-start
  110.6 14.7 %shard_map.96 = (s16[2,16,208,128]{3,2,1,0:T(8,128)(2,1)S(1)}, s16[8,400,128]{2,1,0:T(8,128)(2,1)S(1)}) custom-call(s32[1,1,576]{2,1,0:T(1,128)} %rows_in.3, s32[1,1,576]{2,1,0:T(1,128)} %cols_in.3, s32[1,1]{1,0:T(1,128)S(6)} %copy.10.count_ref, bf16[96,64,128]{2,1,0:T(8,128)(2,1)S(1)} %bitcast.6, bf16[48,64,128]{2,1,0:T(8,128)(2,1)S(1)} %bitcast.8, ...), custom_call_target="tpu_custom_call" | custom-call | flops 9663676416 | bytes 18874368 | tf_op jit(solution)/shard_map/pallas_call | solution.py:568
  125.3 0.0 copy-done
  125.3 36.9 %shard_map.97 = (f32[64,768]{1,0:T(8,128)S(1)}, f32[192,256]{1,0:T(8,128)S(1)}, f32[192,128]{1,0:T(8,128)S(1)}) custom-call(f32[64,768]{1,0:T(8,128)S(1)} %get-tuple-element.21.ortho_ref, f32[64,768]{1,0:T(8,128)S(1)} %get-tuple-element.28.residual_ref.residual_in, f32[64,768]{1,0:T(8,128)S(1)} %copy-done, f32[64,768]{1,0:T(8,128)S(1)} %get-tuple-element.29.image_x_ref, ...), custom_call_target="tpu_custom_call" | custom-call | tf_op jit(solution)/shard_map/pallas_call | solution.py:853
  162.3 1.9 %shard_map.98 = (f32[64,768]{1,0:T(8,128)}, f32[64,768]{1,0:T(8,128)}, f32[192,192]{1,0:T(8,128)}, f32[192,192]{1,0:T(8,128)}) custom-call(f32[64,768]{1,0:T(8,128)S(1)} %get-tuple-element.28.residual_ref.residual_in, f32[64,768]{1,0:T(8,128)S(1)} %get-tuple-element.35.image_in, f32[192,256]{1,0:T(8,128)S(1)} %get-tuple-element.36.early_ref, ...), custom_call_target="tpu_custom_call" | custom-call | tf_op jit(solution)/shard_map/pallas_call | solution.py:872
Async XLA Ops:
  110.6 14.7 %copy-start = (f32[64,768]{1,0:T(8,128)S(1)}, f32[64,768]{1,0:T(8,128)}, u32[]{:S(2)}) copy-start(f32[64,768]{1,0:T(8,128)} %p_ref.3) | copy-start | bytes 589828
